TPU v7x, 32 devices: a whole 2x2x4 slice. The times are simulated.
32 devices in a mesh: src: 4 (over y, x), tgt: 8 (over z, core).
Axes of the slice: x: 2, y: 2, z: 4, core: 2. Of those that a mesh axis runs over, the one named last changes fastest.
Arguments:
- src_emb_t: bfloat16 [300, 4096], P(None, 'src'), may hold values from -6 to 6
- tgt_emb_t: bfloat16 [300, 16384], P(None, 'tgt'), may hold values from -6 to 6
- core: float32 [300, 300], replicated, may hold values from -0.08 to 0.2
- src_logw: float32 [4096], P('src'), may hold values from -1.5 to 1.5
- tgt_logw: float32 [16384], P('tgt'), may hold values from -1.5 to 1.5
Outputs:
- src_potential: float32 [4096], P('src')
- tgt_potential: float32 [16384], P('tgt')
- next_core: float32 [300, 300], replicated
All inputs are finite; a program needn't handle non-finite values.
Results may differ from a plain program's by a relative error of at most 0.0036.
Values sent between devices are 32-bit elements; how exact they have to be, the bound alone decides.
A program may use at most 64 MiB of HBM per device.

v0:
```python
import jax
import jax.numpy as jnp
from jax import lax
from jax.sharding import PartitionSpec as P

D = 300
ITERS = 3


def row_lse(shifted):
    peaks = jnp.max(shifted, axis=1)
    peaks = lax.pmax(peaks, "tgt")
    totals = lax.psum(jnp.sum(jnp.exp(shifted - peaks[:, None]), axis=1), "tgt")
    return peaks + jnp.log(totals)


def col_lse(shifted):
    peaks = jnp.max(shifted, axis=0)
    peaks = lax.pmax(peaks, "src")
    totals = lax.psum(jnp.sum(jnp.exp(shifted - peaks[None, :]), axis=0), "src")
    return peaks + jnp.log(totals)


def per_device(src_emb_t, tgt_emb_t, core, src_logw, tgt_logw):
    projected = jnp.dot(
        core.T, src_emb_t.astype(jnp.float32), precision=lax.Precision.HIGHEST
    ).astype(jnp.bfloat16)

    def scores_of():
        return lax.dot_general(
            projected, tgt_emb_t, (((0,), (0,)), ((), ())), preferred_element_type=jnp.float32
        )

    stored = scores_of()
    tgt_pot = jnp.zeros((tgt_emb_t.shape[1],), jnp.float32)
    src_pot = jnp.zeros((src_emb_t.shape[1],), jnp.float32)
    for step in range(ITERS):
        current = stored if step == 0 else scores_of()
        src_pot = src_logw - row_lse(current + tgt_pot[None, :])
        current = scores_of()
        tgt_pot = tgt_logw - col_lse(current + src_pot[:, None])
    current = scores_of()
    plan = jnp.exp(current + src_pot[:, None] + tgt_pot[None, :]).astype(jnp.bfloat16)
    total_words = src_emb_t.shape[1] * lax.axis_size("src")
    share = src_emb_t.shape[1] // lax.axis_size("tgt")
    portion = lax.psum_scatter(
        lax.dot_general(
            plan, tgt_emb_t, (((1,), (1,)), ((), ())), preferred_element_type=jnp.float32
        ),
        "tgt",
        scatter_dimension=0,
        tiled=True,
    )
    offset = lax.axis_index("tgt") * share
    my_words = lax.dynamic_slice_in_dim(src_emb_t, offset, share, 1)
    partial_core = jnp.dot(my_words.astype(jnp.float32), portion, precision=lax.Precision.HIGHEST)
    summed = lax.psum(partial_core, ("src", "tgt"))
    next_core = summed * (D / total_words)
    return (src_pot, tgt_pot, next_core)


def solution(mesh):
    placed = (P(None, "src"), P(None, "tgt"), P(), P("src"), P("tgt"))
    return jax.shard_map(
        per_device, mesh=mesh, in_specs=placed, out_specs=(P("src"), P("tgt"), P()), check_vma=False
    )
```

profile of v0, /device:TPU:0, one launch (start us, length us, event | category | flops | bytes accessed | tf_op | source)
XLA Modules:
  0.0 379.4 jit_solution(6853388448847303816)
XLA Ops:
  7.2 0.0 reduce-scatter.2.cloned.1.call-start
  7.2 2.5 convolution_convert_fusion
  9.7 5.6 %fusion.6 = (f32[1024]{0:T(1024)S(1)}, f32[1024,2048]{1,0:T(8,128)}) fusion(bf16[300,1024]{1,0:T(8,128)(2,1)S(1)} %convolution_convert_fusion, bf16[300,2048]{1,0:T(8,128)(2,1)S(1)} %copy-done), kind=kOutput, calls=%fused_computation.26 | convolution fusion | flops 1260387328 | bytes 10235904 | tf_op jit(solution)/shard_map/dot_general | solution.py:30
  15.4 18.1 %pmax.42 = f32[1024]{0:T(1024)S(1)} all-reduce(f32[1024]{0:T(1024)S(1)} %get-tuple-element.3), channel_id=1, replica_groups=mesh['src'=4,'tgt'=8] {'tgt'}, use_global_device_ids=true, to_apply=%region_1.0 | all-reduce | flops 1024 | bytes 8192 | tf_op jit(solution)/shard_map/pmax | solution.py:12
  33.4 4.6 %exponential_reduce_fusion.5 = f32[1024]{0:T(1024)S(1)} fusion(f32[1024,2048]{1,0:T(8,128)} %get-tuple-element.4, f32[1024]{0:T(1024)S(1)} %pmax.42), kind=kLoop, calls=%fused_computation.6 | loop fusion | flops 4193280 | bytes 8396800 | tf_op jit(solution)/shard_map/reduce_sum | solution.py:13
  38.0 13.6 %psum.49 = f32[1024]{0:T(1024)S(1)} all-reduce(f32[1024]{0:T(1024)S(1)} %exponential_reduce_fusion.5), channel_id=1, replica_groups=mesh['src'=4,'tgt'=8] {'tgt'}, use_global_device_ids=true, to_apply=%region_3.0 | all-reduce | flops 1024 | bytes 8192 | tf_op jit(solution)/shard_map/psum | solution.py:13
  51.7 4.0 %add_reduce_fusion.3 = f32[2048]{0:T(1024)S(1)} fusion(f32[1024,2048]{1,0:T(8,128)} %get-tuple-element.4, f32[1024]{0:T(1024)S(1)} %add_subtract_fusion.5), kind=kLoop, calls=%fused_computation.10 | loop fusion | flops 4192256 | bytes 8400896 | tf_op jit(solution)/shard_map/reduce_max | solution.py:18
  55.7 10.1 %pmax.43 = f32[2048]{0:T(1024)S(1)} all-reduce(f32[2048]{0:T(1024)S(1)} %add_reduce_fusion.3), channel_id=1, replica_groups=mesh['src'=4,'tgt'=8] {'src'}, use_global_device_ids=true, to_apply=%region_5.0 | all-reduce | flops 2048 | bytes 16384 | tf_op jit(solution)/shard_map/pmax | solution.py:19
  65.8 4.3 %exponential_reduce_fusion.4 = f32[2048]{0:T(1024)S(1)} fusion(f32[1024,2048]{1,0:T(8,128)} %get-tuple-element.4, f32[2048]{0:T(1024)S(1)} %pmax.43, f32[1024]{0:T(1024)S(1)} %add_subtract_fusion.5), kind=kLoop, calls=%fused_computation.5 | loop fusion | flops 6289408 | bytes 8409088 | tf_op jit(solution)/shard_map/reduce_sum | solution.py:20
  70.1 8.1 %psum.50 = f32[2048]{0:T(1024)S(1)} all-reduce(f32[2048]{0:T(1024)S(1)} %exponential_reduce_fusion.4), channel_id=1, replica_groups=mesh['src'=4,'tgt'=8] {'src'}, use_global_device_ids=true, to_apply=%region_7.0 | all-reduce | flops 2048 | bytes 16384 | tf_op jit(solution)/shard_map/psum | solution.py:20
  78.2 4.0 %add_reduce_fusion.2 = f32[1024]{0:T(1024)S(1)} fusion(f32[1024,2048]{1,0:T(8,128)} %get-tuple-element.4, f32[2048]{0:T(1024)S(1)} %add_subtract_fusion.2), kind=kLoop, calls=%fused_computation.9 | loop fusion | flops 4193280 | bytes 8400896 | tf_op jit(solution)/shard_map/reduce_max | solution.py:11
  82.2 13.6 %pmax.44 = f32[1024]{0:T(1024)S(1)} all-reduce(f32[1024]{0:T(1024)S(1)} %add_reduce_fusion.2), channel_id=1, replica_groups=mesh['src'=4,'tgt'=8] {'tgt'}, use_global_device_ids=true, to_apply=%region_9.0 | all-reduce | flops 1024 | bytes 8192 | tf_op jit(solution)/shard_map/pmax | solution.py:12
  95.8 4.4 %exponential_reduce_fusion.3 = f32[1024]{0:T(1024)S(1)} fusion(f32[1024,2048]{1,0:T(8,128)} %get-tuple-element.4, f32[1024]{0:T(1024)S(1)} %pmax.44, f32[2048]{0:T(1024)S(1)} %add_subtract_fusion.2), kind=kLoop, calls=%fused_computation.4 | loop fusion | flops 6290432 | bytes 8404992 | tf_op jit(solution)/shard_map/reduce_sum | solution.py:13
  100.2 13.6 %psum.51 = f32[1024]{0:T(1024)S(1)} all-reduce(f32[1024]{0:T(1024)S(1)} %exponential_reduce_fusion.3), channel_id=1, replica_groups=mesh['src'=4,'tgt'=8] {'tgt'}, use_global_device_ids=true, to_apply=%region_11.0 | all-reduce | flops 1024 | bytes 8192 | tf_op jit(solution)/shard_map/psum | solution.py:13
  113.8 4.0 %add_reduce_fusion.1 = f32[2048]{0:T(1024)S(1)} fusion(f32[1024,2048]{1,0:T(8,128)} %get-tuple-element.4, f32[1024]{0:T(1024)S(1)} %add_subtract_fusion.4), kind=kLoop, calls=%fused_computation.8 | loop fusion | flops 4192256 | bytes 8400896 | tf_op jit(solution)/shard_map/reduce_max | solution.py:18
  117.8 9.1 %pmax.45 = f32[2048]{0:T(1024)S(1)} all-reduce(f32[2048]{0:T(1024)S(1)} %add_reduce_fusion.1), channel_id=1, replica_groups=mesh['src'=4,'tgt'=8] {'src'}, use_global_device_ids=true, to_apply=%region_13.0 | all-reduce | flops 2048 | bytes 16384 | tf_op jit(solution)/shard_map/pmax | solution.py:19
  127.0 4.3 %exponential_reduce_fusion.2 = f32[2048]{0:T(1024)S(1)} fusion(f32[1024,2048]{1,0:T(8,128)} %get-tuple-element.4, f32[2048]{0:T(1024)S(1)} %pmax.45, f32[1024]{0:T(1024)S(1)} %add_subtract_fusion.4), kind=kLoop, calls=%fused_computation.3 | loop fusion | flops 6289408 | bytes 8409088 | tf_op jit(solution)/shard_map/reduce_sum | solution.py:20
  131.3 8.2 %psum.52 = f32[2048]{0:T(1024)S(1)} all-reduce(f32[2048]{0:T(1024)S(1)} %exponential_reduce_fusion.2), channel_id=1, replica_groups=mesh['src'=4,'tgt'=8] {'src'}, use_global_device_ids=true, to_apply=%region_15.0 | all-reduce | flops 2048 | bytes 16384 | tf_op jit(solution)/shard_map/psum | solution.py:20
  139.5 4.0 %add_reduce_fusion = f32[1024]{0:T(1024)S(1)} fusion(f32[1024,2048]{1,0:T(8,128)} %get-tuple-element.4, f32[2048]{0:T(1024)S(1)} %add_subtract_fusion.1), kind=kLoop, calls=%fused_computation.7 | loop fusion | flops 4193280 | bytes 8400896 | tf_op jit(solution)/shard_map/reduce_max | solution.py:11
  143.6 13.8 %pmax.46 = f32[1024]{0:T(1024)S(1)} all-reduce(f32[1024]{0:T(1024)S(1)} %add_reduce_fusion), channel_id=1, replica_groups=mesh['src'=4,'tgt'=8] {'tgt'}, use_global_device_ids=true, to_apply=%region_17.0 | all-reduce | flops 1024 | bytes 8192 | tf_op jit(solution)/shard_map/pmax | solution.py:12
  157.3 4.4 %exponential_reduce_fusion.1 = f32[1024]{0:T(1024)S(1)} fusion(f32[1024,2048]{1,0:T(8,128)} %get-tuple-element.4, f32[1024]{0:T(1024)S(1)} %pmax.46, f32[2048]{0:T(1024)S(1)} %add_subtract_fusion.1), kind=kLoop, calls=%fused_computation.2 | loop fusion | flops 6290432 | bytes 8404992 | tf_op jit(solution)/shard_map/reduce_sum | solution.py:13
  161.7 13.6 %psum.53 = f32[1024]{0:T(1024)S(1)} all-reduce(f32[1024]{0:T(1024)S(1)} %exponential_reduce_fusion.1), channel_id=1, replica_groups=mesh['src'=4,'tgt'=8] {'tgt'}, use_global_device_ids=true, to_apply=%region_19.0 | all-reduce | flops 1024 | bytes 8192 | tf_op jit(solution)/shard_map/psum | solution.py:13
  175.3 4.0 %add_reduce_fusion.4 = f32[2048]{0:T(1024)S(1)} fusion(f32[1024,2048]{1,0:T(8,128)} %get-tuple-element.4, f32[1024]{0:T(1024)S(1)} %add_subtract_fusion.3), kind=kLoop, calls=%fused_computation.11 | loop fusion | flops 4192256 | bytes 8400896 | tf_op jit(solution)/shard_map/reduce_max | solution.py:18
  179.4 9.8 %pmax.47 = f32[2048]{0:T(1024)S(1)} all-reduce(f32[2048]{0:T(1024)S(1)} %add_reduce_fusion.4), channel_id=1, replica_groups=mesh['src'=4,'tgt'=8] {'src'}, use_global_device_ids=true, to_apply=%region_21.0 | all-reduce | flops 2048 | bytes 16384 | tf_op jit(solution)/shard_map/pmax | solution.py:19
  189.1 4.3 %exponential_reduce_fusion = f32[2048]{0:T(1024)S(1)} fusion(f32[1024,2048]{1,0:T(8,128)} %get-tuple-element.4, f32[2048]{0:T(1024)S(1)} %pmax.47, f32[1024]{0:T(1024)S(1)} %add_subtract_fusion.3), kind=kLoop, calls=%fused_computation.1 | loop fusion | flops 6289408 | bytes 8409088 | tf_op jit(solution)/shard_map/reduce_sum | solution.py:20
  193.4 8.3 %psum.54 = f32[2048]{0:T(1024)S(1)} all-reduce(f32[2048]{0:T(1024)S(1)} %exponential_reduce_fusion), channel_id=1, replica_groups=mesh['src'=4,'tgt'=8] {'src'}, use_global_device_ids=true, to_apply=%region_23.0 | all-reduce | flops 2048 | bytes 16384 | tf_op jit(solution)/shard_map/psum | solution.py:20
  201.8 7.0 %fusion = f32[1024,300]{1,0:T(8,128)} fusion(bf16[300,2048]{1,0:T(8,128)(2,1)S(1)} %copy-done, f32[1024,2048]{1,0:T(8,128)} %get-tuple-element.4, f32[2048]{0:T(1024)S(1)} %add_subtract_fusion, f32[1024]{0:T(1024)S(1)} %add_subtract_fusion.3), kind=kOutput, calls=%fused_computation.12 | convolution fusion | flops 1264582656 | bytes 10858496 | tf_op jit(solution)/shard_map/dot_general | solution.py:47
  208.8 0.0 all-reduce.2.cloned.1.call-start
  208.9 31.5 %reduce-scatter.2.cloned.1.call-done = f32[128,300]{1,0:T(8,128)} async-done(((f32[1024,300]{1,0:T(8,128)}), f32[128,300]{1,0:T(8,128)}) %reduce-scatter.2.cloned.1.call-update) | async-done | bytes 153616 | tf_op jit(solution)/shard_map/reduce_scatter | solution.py:46
  240.4 2.1 fusion.3
  242.5 128.3 %all-reduce.2.cloned.1.call-done = f32[300,300]{1,0:T(8,128)} async-done(((f32[300,300]{1,0:T(8,128)}), f32[300,300]{1,0:T(8,128)}) %all-reduce.2.cloned.1.call-update) | async-done | bytes 360016 | tf_op jit(solution)/shard_map/psum | solution.py:57
  370.8 1.8 broadcast_multiply_fusion
  (18 shorter events, 0.1 us)
Async XLA Ops:
  7.2 2.5 copy-start
  7.2 233.2 %reduce-scatter.2.cloned.1.call-start = ((), (), s32[]{:S(2)}) async-start(), calls=%async_computation.1 | async-start | bytes 1769472 | tf_op jit(solution)/shard_map/reduce_scatter | solution.py:46
  9.7 41.9 %copy-start.3 = (f32[1024]{0:T(1024)S(1)}, f32[1024]{0:T(1024)}, u32[]{:S(2)}) copy-start(f32[1024]{0:T(1024)} %param.8) | copy-start | bytes 12292
  51.7 26.5 %copy-start.1 = (f32[2048]{0:T(1024)S(1)}, f32[2048]{0:T(1024)}, u32[]{:S(2)}) copy-start(f32[2048]{0:T(1024)} %param.9) | copy-start | bytes 24580
  175.3 26.4 %copy-start.2 = (f32[1024]{0:T(1024)}, f32[1024]{0:T(1024)S(1)}, u32[]{:S(2)}) copy-start(f32[1024]{0:T(1024)S(1)} %add_subtract_fusion.3) | copy-start | bytes 12292
  201.8 7.0 %copy-start.4 = (f32[2048]{0:T(1024)}, f32[2048]{0:T(1024)S(1)}, u32[]{:S(2)}) copy-start(f32[2048]{0:T(1024)S(1)} %add_subtract_fusion) | copy-start | bytes 24580
  208.8 162.0 %all-reduce.2.cloned.1.call-start = ((), (), s32[]{:S(2)}) async-start(), calls=%async_computation.2 | async-start | bytes 933888 | tf_op jit(solution)/shard_map/psum | solution.py:57
Sparse Core Ops, SparseCore 0:
  208.9 31.4 reduce-scatter.1
  246.3 124.4 all-reduce.1
where the time goes:
time: 380 us; the launch traced here: 379 us
  waiting for transfers between devices  160 us (42%)
  blocking collectives  140 us (37%)
  other arithmetic  48.2 us (13%)
  matrix products  17.2 us (5%)
  between operations  14.3 us (4%)
    psum x1, waiting for transfers between devices, per_device(): summed = lax.psum(partial_core, ('src', 'tgt'))  128 us
    pmax x3, blocking collectives, row_lse(): peaks = lax.pmax(peaks, 'tgt')  45.4 us
    psum x3, blocking collectives, row_lse(): totals = lax.psum(jnp.sum(jnp.exp(shifted - peaks[:, None]), axis=1), 'tgt')  40.8 us
    reduce_scatter x1, waiting for transfers between devices, per_device(): lax.psum_scatter(lax.dot_general(plan, tgt_emb_t, (((1,), (1,)), ((), ())...  31.5 us
    pmax x3, blocking collectives, col_lse(): peaks = lax.pmax(peaks, 'src')  29 us
    psum x3, blocking collectives, col_lse(): totals = lax.psum(jnp.sum(jnp.exp(shifted - peaks[None, :]), axis=0), 'src')  24.6 us
    reduce_sum x3, other arithmetic, row_lse(): totals = lax.psum(jnp.sum(jnp.exp(shifted - peaks[:, None]), axis=1), 'tgt')  13.4 us
    reduce_sum x3, other arithmetic, col_lse(): totals = lax.psum(jnp.sum(jnp.exp(shifted - peaks[None, :]), axis=0), 'src')  12.9 us
  transfers between devices with their start and end apart: 2, of which 2 were waited for; matrix products, arithmetic and copies ran while one was open for 0% of the time, Pallas kernels for 0%

commit v1 on v0

v1 whole, which is shorter than its diff:
```python
import functools
import math

import jax
import jax.numpy as jnp
from jax import lax
from jax.experimental import pallas as pl
from jax.experimental.pallas import tpu as pltpu
from jax.sharding import PartitionSpec as P

ITERS = 3
LOG2E = 1.4426950408889634
LN2 = 0.6931471805599453
LANES = 128
SHIFT = 60.0
MESH = pl.DeviceIdType.MESH


def tile(t):
    return slice(t * LANES, (t + 1) * LANES)


def kernel(
    n_src, n_tgt,
    src_ref, tgt_ref, core_ref, slw_ref, tlw_ref,
    f_out, g_out, core_out,
    S, proj, M, T, FB, FS, GS, RXF, RXG, plan, CB, RX1, RX2, RX3, OUT,
    fsend, frecv, gsend, grecv, s1, r1, s2, r2, s3, r3, s4, r4, s5, r5, s6, r6,
):
    si, ti = lax.axis_index("src"), lax.axis_index("tgt")
    dim, rows = src_ref.shape
    cols = tgt_ref.shape[1]
    rc, cc = rows // LANES, cols // LANES
    f32, bf16 = jnp.float32, jnp.bfloat16

    def src_peers():
        return [lax.rem(si + k, n_src) for k in range(1, n_src)]

    def tgt_peers():
        return [lax.rem(ti + k, n_tgt) for k in range(1, n_tgt)]

    barrier = pltpu.get_barrier_semaphore()
    for p in src_peers():
        pl.semaphore_signal(barrier, inc=1, device_id=(p, ti), device_id_type=MESH)
    for p in tgt_peers():
        pl.semaphore_signal(barrier, inc=1, device_id=(si, p), device_id_type=MESH)

    c32 = core_ref[...]
    c0 = c32.astype(bf16)
    left = c32 - c0.astype(f32)
    c1 = left.astype(bf16)
    c2 = (left - c1.astype(f32)).astype(bf16)
    src = src_ref[...]

    def contract(a, b, da, db):
        return lax.dot_general(a, b, (((da,), (db,)), ((), ())), preferred_element_type=f32)

    proj[...] = (
        contract(src, c0, 0, 0) + (contract(src, c1, 0, 0) + contract(src, c2, 0, 0))
    ).astype(bf16)

    M[...] = jnp.full((rows, LANES), -jnp.inf, f32)
    wide = 2 * LANES

    def score_tile(t, carry):
        at = pl.ds(pl.multiple_of(t * wide, wide), wide)
        y = jnp.dot(proj[...], tgt_ref[:, at], preferred_element_type=f32) * LOG2E
        S[:, at] = y
        M[...] = jnp.maximum(M[...], jnp.maximum(y[:, :LANES], y[:, LANES:]))
        return carry

    lax.fori_loop(0, cols // wide, score_tile, 0)

    def groups(body, carry, unroll):
        def step(i, carry):
            for k in range(unroll):
                carry = body(pl.ds(pl.multiple_of((i * unroll + k) * 8, 8), 8), carry)
            return carry

        return lax.fori_loop(0, rows // (8 * unroll), step, carry)

    def first_rows(r, carry):
        m = M[r, :]
        parts = [jnp.exp2(S[r, tile(t)] - m) for t in range(cc)]
        while len(parts) > 1:
            parts = [a + b for a, b in zip(parts[::2], parts[1::2])]
        T[r, :] = parts[0]
        return carry

    groups(first_rows, 0, 4)

    def broadcast_down(line):
        return jnp.broadcast_to(line, (8, LANES))

    def to_columns(dense):
        for c in range(rc):
            FB[tile(c), :] = jnp.broadcast_to(dense[c : c + 1, :], (LANES, LANES)).T

    def exchange(buf, step, me, peers, send, recv, where):
        copies = []
        for k, p in enumerate(peers):
            copy = pltpu.make_async_remote_copy(
                src_ref=buf.at[step, me],
                dst_ref=buf.at[step, me],
                send_sem=send.at[step, k],
                recv_sem=recv.at[step, me],
                device_id=where(p),
                device_id_type=MESH,
            )
            copy.start()
            copies.append(copy)
        for k, p in enumerate(peers):
            pltpu.make_async_remote_copy(
                src_ref=buf.at[step, p],
                dst_ref=buf.at[step, p],
                send_sem=send.at[step, k],
                recv_sem=recv.at[step, p],
                device_id=where(p),
                device_id_type=MESH,
            ).wait_recv()
        return copies

    def share_rows(step):
        RXF[step, ti] = FS[...]
        return exchange(RXF, step, ti, tgt_peers(), fsend, frecv, lambda p: (si, p))

    def share_cols(step):
        RXG[step, si] = GS[...]
        return exchange(RXG, step, si, src_peers(), gsend, grecv, lambda p: (p, ti))

    def lse_of(buf, step, n):
        parts = [buf[step, k] for k in range(n)]
        top = functools.reduce(jnp.maximum, parts)
        return top + jnp.log2(sum(jnp.exp2(x - top) for x in parts))

    pending = []
    slw = slw_ref[...] * LOG2E
    tlw = tlw_ref[...] * LOG2E

    for c in range(rc):
        mt, st = M[tile(c), :].T, T[tile(c), :].T
        top = jnp.max(mt, axis=0, keepdims=True)
        FS[c : c + 1, :] = top + jnp.log2(jnp.sum(st * jnp.exp2(mt - top), axis=0, keepdims=True))
    pl.semaphore_wait(barrier, (n_src - 1) + (n_tgt - 1))
    pending += share_rows(0)
    f1 = slw - lse_of(RXF, 0, n_tgt)
    to_columns(f1)

    def peak_cols(r, acc):
        fb = FB[r, :]
        return tuple(jnp.maximum(a, S[r, tile(t)] + fb) for t, a in enumerate(acc))

    acc = groups(peak_cols, tuple(jnp.full((8, LANES), -jnp.inf, f32) for t in range(cc)), 4)
    for t in range(cc):
        GS[t : t + 1, :] = jnp.max(acc[t], axis=0, keepdims=True)
    cm = GS[...]
    less = [broadcast_down(SHIFT - cm[t : t + 1, :]) for t in range(cc)]

    def first_cols(r, acc):
        fb = FB[r, :]
        new = []
        for t, a in enumerate(acc):
            e = jnp.exp2(S[r, tile(t)] + fb + less[t])
            S[r, tile(t)] = e
            new.append(a + e)
        return tuple(new)

    zeros = tuple(jnp.zeros((8, LANES), f32) for t in range(cc))
    acc = groups(first_cols, zeros, 2)
    for t in range(cc):
        GS[t : t + 1, :] = jnp.sum(acc[t], axis=0, keepdims=True)
    GS[...] = cm + (jnp.log2(GS[...]) - SHIFT)
    pending += share_cols(0)
    g = tlw - lse_of(RXG, 0, n_src)
    v = jnp.exp2(cm + g)

    for step in range(1, ITERS):
        vb = [broadcast_down(v[t : t + 1, :]) for t in range(cc)]

        def later_rows(r, carry):
            parts = [S[r, tile(t)] * vb[t] for t in range(cc)]
            while len(parts) > 1:
                parts = [a + b for a, b in zip(parts[::2], parts[1::2])]
            T[r, :] = parts[0]
            return carry

        groups(later_rows, 0, 4)
        for c in range(rc):
            FS[c : c + 1, :] = jnp.sum(T[tile(c), :].T, axis=0, keepdims=True)
        pending += share_rows(step)
        move = slw + (SHIFT - jnp.log2(sum(RXF[step, k] for k in range(n_tgt))))
        u = jnp.exp2(move)
        to_columns(u)

        def later_cols(r, acc):
            ub = FB[r, :]
            return tuple(a + S[r, tile(t)] * ub for t, a in enumerate(acc))

        acc = groups(later_cols, zeros, 4)
        for t in range(cc):
            GS[t : t + 1, :] = jnp.sum(acc[t], axis=0, keepdims=True)
        GS[...] = GS[...] * v
        pending += share_cols(step)
        g = g + (tlw + (SHIFT - jnp.log2(sum(RXG[step, k] for k in range(n_src)))))
        v = jnp.exp2(cm + g)

    f_out[...] = (f1 + move) * LN2
    g_out[...] = g * LN2

    to_columns(u * (2.0 ** -SHIFT))
    tall = plan.shape[0]
    tgt = tgt_ref[...]
    total = None
    for c in range(rows // tall):
        at = slice(c * tall, (c + 1) * tall)
        ub = FB[at, :]
        for t in range(cc):
            plan[:, tile(t)] = (S[at, tile(t)] * ub * v[t : t + 1, :]).astype(bf16)
        panel = contract(plan[...], tgt, 1, 1)
        high = panel.astype(bf16)
        low = (panel - high.astype(f32)).astype(bf16)
        words = src_ref[:, at]
        part = jnp.dot(words, high, preferred_element_type=f32) + jnp.dot(
            words, low, preferred_element_type=f32
        )
        total = part if total is None else total + part

    full, rest = dim // LANES, dim % LANES
    line = -(-dim // 8) * 8
    short = -(-rest // 8) * 8
    CB[...] = jnp.zeros(CB.shape, f32)
    for t in range(full):
        CB[t * line : t * line + dim, :] = total[:, tile(t)]
    if rest:
        plan_rows = -(-dim // LANES) * LANES
        S[0:plan_rows, 0:LANES] = jnp.zeros((plan_rows, LANES), f32)
        S[0:dim, 0:rest] = total[:, full * LANES :]
        for k in range(plan_rows // LANES):
            base = full * line + k * short
            CB[base : base + short, :] = S[tile(k), 0:LANES].T[0:short, :]

    height = CB.shape[0]
    core_id, zi, nz = lax.rem(ti, 2), lax.div(ti, 2), n_tgt // 2
    half = height // 2
    quart = half // n_src
    piece = quart // nz
    half_at = core_id * half
    quart_at = half_at + si * quart
    piece_at = quart_at + zi * piece

    def span(start, size):
        return pl.ds(pl.multiple_of(start, 8), size)

    def remote(source, dest, send, recv, where):
        return pltpu.make_async_remote_copy(
            src_ref=source, dst_ref=dest, send_sem=send, recv_sem=recv,
            device_id=where, device_id_type=MESH,
        )

    mate = (si, zi * 2 + (1 - core_id))
    z_peers = [lax.rem(zi + k, nz) for k in range(1, nz)]
    on_z = lambda p: (si, p * 2 + core_id)
    on_src = lambda p: (p, ti)

    copy = remote(CB.at[span((1 - core_id) * half, half)], RX1, s1, r1, mate)
    copy.start()
    copy.wait_recv()
    pending.append(copy)
    CB[span(half_at, half), :] += RX1[...]

    def scatter(n, me, peers, base, size, RX, send, recv, where):
        for k, p in enumerate(peers):
            copy = remote(CB.at[span(base + p * size, size)], RX.at[me], send.at[k], recv.at[me], where(p))
            copy.start()
            pending.append(copy)
        for k, p in enumerate(peers):
            remote(RX.at[p], RX.at[p], send.at[k], recv.at[p], where(p)).wait_recv()
        own = CB[span(base + me * size, size), :]
        for p in peers:
            own = own + RX[p]
        return own

    CB[span(quart_at, quart), :] = scatter(n_src, si, src_peers(), half_at, quart, RX2, s2, r2, on_src)
    OUT[span(piece_at, piece), :] = scatter(nz, zi, z_peers, quart_at, piece, RX3, s3, r3, on_z)

    def gather(me, peers, base, size, send, recv, where):
        for k, p in enumerate(peers):
            at = span(base + me * size, size)
            copy = remote(OUT.at[at], OUT.at[at], send.at[k], recv.at[me], where(p))
            copy.start()
            pending.append(copy)
        for k, p in enumerate(peers):
            at = span(base + p * size, size)
            remote(OUT.at[at], OUT.at[at], send.at[k], recv.at[p], where(p)).wait_recv()

    gather(zi, z_peers, quart_at, piece, s4, r4, on_z)
    gather(si, src_peers(), half_at, quart, s5, r5, on_src)
    gather(core_id, [1 - core_id], 0, half, s6, r6, lambda p: mate)

    scale = dim / (rows * n_src)
    for t in range(full):
        core_out[:, tile(t)] = OUT[t * line : t * line + dim, :] * scale
    if rest:
        for k in range(-(-dim // LANES)):
            base = full * line + k * short
            CB_rows = jnp.concatenate(
                [OUT[base : base + short, :], jnp.zeros((LANES - short, LANES), f32)], axis=0
            ).T * scale
            count = min(LANES, dim - k * LANES)
            core_out[k * LANES : k * LANES + count, full * LANES :] = CB_rows[0:count, 0:rest]

    for copy in pending:
        copy.wait_send()


def per_device(n_src, n_tgt, src_emb_t, tgt_emb_t, core, src_logw, tgt_logw):
    dim, rows = src_emb_t.shape
    cols = tgt_emb_t.shape[1]
    f32 = jnp.float32
    line, short = -(-dim // 8) * 8, -(-(dim % LANES) // 8) * 8
    need = (dim // LANES) * line + -(-dim // LANES) * short
    step = 8 * n_src * n_tgt
    height = -(-need // step) * step
    half = height // 2
    quart = half // n_src
    nz = n_tgt // 2
    sems = pltpu.SemaphoreType.DMA
    vmem = pl.BlockSpec(memory_space=pltpu.VMEM)
    rc, cc = rows // LANES, cols // LANES
    f, g, new = pl.pallas_call(
        functools.partial(kernel, n_src, n_tgt),
        out_shape=(
            jax.ShapeDtypeStruct((rc, LANES), f32),
            jax.ShapeDtypeStruct((cc, LANES), f32),
            jax.ShapeDtypeStruct((dim, dim), f32),
        ),
        in_specs=[vmem] * 5,
        out_specs=(vmem,) * 3,
        scratch_shapes=[
            pltpu.VMEM((rows, cols), f32),
            pltpu.VMEM((rows, dim), jnp.bfloat16),
            pltpu.VMEM((rows, LANES), f32),
            pltpu.VMEM((rows, LANES), f32),
            pltpu.VMEM((rows, LANES), f32),
            pltpu.VMEM((rc, LANES), f32),
            pltpu.VMEM((cc, LANES), f32),
            pltpu.VMEM((ITERS, n_tgt, rc, LANES), f32),
            pltpu.VMEM((ITERS, n_src, cc, LANES), f32),
            pltpu.VMEM((256, cols), jnp.bfloat16),
            pltpu.VMEM((height, LANES), f32),
            pltpu.VMEM((half, LANES), f32),
            pltpu.VMEM((n_src, quart, LANES), f32),
            pltpu.VMEM((nz, quart // nz, LANES), f32),
            pltpu.VMEM((height, LANES), f32),
            sems((ITERS, n_tgt)), sems((ITERS, n_tgt)),
            sems((ITERS, n_src)), sems((ITERS, n_src)),
            sems, sems,
            sems((n_src,)), sems((n_src,)),
            sems((nz,)), sems((nz,)),
            sems((nz,)), sems((nz,)),
            sems((n_src,)), sems((n_src,)),
            sems((2,)), sems((2,)),
        ],
        compiler_params=pltpu.CompilerParams(
            collective_id=0, has_side_effects=True, vmem_limit_bytes=48 * 1024 * 1024
        ),
    )(src_emb_t, tgt_emb_t, core, src_logw.reshape(rc, LANES), tgt_logw.reshape(cc, LANES))
    return f.reshape(rows), g.reshape(cols), new


def solution(mesh):
    placed = (P(None, "src"), P(None, "tgt"), P(), P("src"), P("tgt"))
    body = functools.partial(per_device, mesh.shape["src"], mesh.shape["tgt"])
    return jax.shard_map(
        body, mesh=mesh, in_specs=placed, out_specs=(P("src"), P("tgt"), P()), check_vma=False
    )
```

time: 380 us -> 68.2 us (0.18)
  waiting for transfers between devices: 160 us -> 0 us
  blocking collectives: 140 us -> 0 us
  Pallas kernels: 0 us -> 60.4 us
  other arithmetic: 48.2 us -> 0 us
  matrix products: 17.2 us -> 0 us
  between operations: 14.3 us -> 0.65 us
  local copies, waits for them, and re-layouts: 0.03 us -> 6.73 us
    psum x1 -> x0, waiting for transfers between devices: 128 us -> none  [per_device(): summed = lax.psum(partial_core, ('src', 'tgt'))]
    pmax x6 -> x0, blocking collectives: 74.4 us -> none  [the longest x3 45.4 us: row_lse(): peaks = lax.pmax(peaks, 'tgt')]
    psum x6 -> x0, blocking collectives: 65.4 us -> none  [the longest x3 40.8 us: row_lse(): totals = lax.psum(jnp.sum(jnp.exp(shifted - peaks[:, None]), axis=1), 'tgt')]
    pallas_call x0 -> x1, Pallas kernels: none -> 60.4 us  [per_device(): pl.pallas_call(functools.partial(kernel, n_src, n_tgt), out_shape=(jax.Sh...]
    reduce_scatter x1 -> x0, waiting for transfers between devices: 31.5 us -> none  [per_device(): lax.psum_scatter(lax.dot_general(plan, tgt_emb_t, (((1,), (1,)), ((), ())...]
    reduce_sum x6 -> x0, other arithmetic: 26.3 us -> none  [the longest x3 13.4 us: row_lse(): totals = lax.psum(jnp.sum(jnp.exp(shifted - peaks[:, None]), axis=1), 'tgt')]
    reduce_max x5 -> x0, other arithmetic: 20.1 us -> none  [the longest x3 12 us: col_lse(): peaks = jnp.max(shifted, axis=0)]
    dot_general x4 -> x0, matrix products: 17.2 us -> none  [the longest x1 7 us: per_device(): lax.dot_general(plan, tgt_emb_t, (((1,), (1,)), ((), ())), preferred_elem...]
  transfers between devices with their start and end apart: 2 -> 0, of which waited for: 2 -> 0; matrix products, arithmetic and copies ran while one was open for 0% -> 0% of each run, Pallas kernels for 0% -> 0%
where the time goes in v1:
time: 68.2 us; the launch traced here: 67.8 us
  Pallas kernels  60.4 us (89%)
  local copies, waits for them, and re-layouts  6.73 us (10%)
    pallas_call x1, Pallas kernels, per_device(): pl.pallas_call(functools.partial(kernel, n_src, n_tgt), out_shape=(jax.Sh...  60.4 us
    unnamed x13, local copies, waits for them, and re-layouts  6.73 us

profile of v1, /device:TPU:0, one launch (start us, length us, event | category | flops | bytes accessed | tf_op | source)
XLA Modules:
  0.0 67.8 jit_solution(17738270789042875531)
XLA Ops:
  0.6 0.0 copy-start
  0.6 1.3 %copy-done = bf16[300,2048]{1,0:T(8,128)(2,1)S(1)} copy-done((bf16[300,2048]{1,0:T(8,128)(2,1)S(1)}, bf16[300,2048]{1,0:T(8,128)(2,1)}, u32[]{:S(2)}) %copy-start) | copy-done | bytes 1228824
  1.9 0.0 copy-start.1
  1.9 1.1 %copy-done.1 = bf16[300,1024]{1,0:T(8,128)(2,1)S(1)} copy-done((bf16[300,1024]{1,0:T(8,128)(2,1)S(1)}, bf16[300,1024]{1,0:T(8,128)(2,1)}, u32[]{:S(2)}) %copy-start.1) | copy-done | bytes 614424
  3.0 0.0 copy-start.2
  3.0 1.0 %copy-done.2 = f32[300,300]{1,0:T(8,128)S(1)} copy-done((f32[300,300]{1,0:T(8,128)S(1)}, f32[300,300]{1,0:T(8,128)}, u32[]{:S(2)}) %copy-start.2) | copy-done | bytes 360024
  4.0 0.0 copy-start.3
  4.0 0.7 %copy-done.3 = f32[2048]{0:T(1024)S(1)} copy-done((f32[2048]{0:T(1024)S(1)}, f32[2048]{0:T(1024)}, u32[]{:S(2)}) %copy-start.3) | copy-done | bytes 8216
  4.7 0.0 copy-start.4
  4.7 0.7 %copy-done.4 = f32[1024]{0:T(1024)S(1)} copy-done((f32[1024]{0:T(1024)S(1)}, f32[1024]{0:T(1024)}, u32[]{:S(2)}) %copy-start.4) | copy-done | bytes 4120
  5.4 60.4 %shard_map.76 = (f32[8,128]{1,0:T(8,128)S(1)}, f32[16,128]{1,0:T(8,128)S(1)}, f32[300,300]{1,0:T(8,128)S(1)}) custom-call(bf16[300,1024]{1,0:T(8,128)(2,1)S(1)} %copy-done.1, bf16[300,2048]{1,0:T(8,128)(2,1)S(1)} %copy-done, f32[300,300]{1,0:T(8,128)S(1)} %copy-done.2, f32[8,128]{1,0:T(8,128)S(1)} %bitcast.6, f32[16,128]{1,0:T(8,128)S(1)} %bitcast.4), custom_call_target="tpu_custom_call" | custom-call | tf_op jit(solution)/shard_map/pallas_call | solution.py:330
  65.8 0.6 copy.11
  66.4 0.6 copy.12
  67.0 0.8 %copy.13 = f32[300,300]{1,0:T(8,128)} copy(f32[300,300]{1,0:T(8,128)S(1)} %get-tuple-element.14) | data formatting | bytes 720000
Async XLA Ops:
  0.6 1.3 %copy-start = (bf16[300,2048]{1,0:T(8,128)(2,1)S(1)}, bf16[300,2048]{1,0:T(8,128)(2,1)}, u32[]{:S(2)}) copy-start(bf16[300,2048]{1,0:T(8,128)(2,1)} %tgt_ref.1) | copy-start | bytes 3686404
  1.9 1.1 %copy-start.1 = (bf16[300,1024]{1,0:T(8,128)(2,1)S(1)}, bf16[300,1024]{1,0:T(8,128)(2,1)}, u32[]{:S(2)}) copy-start(bf16[300,1024]{1,0:T(8,128)(2,1)} %src_ref.1) | copy-start | bytes 1843204
  3.0 1.0 %copy-start.2 = (f32[300,300]{1,0:T(8,128)S(1)}, f32[300,300]{1,0:T(8,128)}, u32[]{:S(2)}) copy-start(f32[300,300]{1,0:T(8,128)} %core_ref.1) | copy-start | bytes 1080004
  4.0 0.7 %copy-start.3 = (f32[2048]{0:T(1024)S(1)}, f32[2048]{0:T(1024)}, u32[]{:S(2)}) copy-start(f32[2048]{0:T(1024)} %param.9) | copy-start | bytes 24580
  4.7 0.7 %copy-start.4 = (f32[1024]{0:T(1024)S(1)}, f32[1024]{0:T(1024)}, u32[]{:S(2)}) copy-start(f32[1024]{0:T(1024)} %param.8) | copy-start | bytes 12292

commit v2 on v1

--- a/solution.py
+++ b/solution.py
@@ -1,5 +1,4 @@
 import functools
-import math
 
 import jax
 import jax.numpy as jnp
@@ -22,9 +21,10 @@
 
 def kernel(
     n_src, n_tgt,
-    src_ref, tgt_ref, core_ref, slw_ref, tlw_ref,
-    f_out, g_out, core_out,
-    S, proj, M, T, FB, FS, GS, RXF, RXG, plan, CB, RX1, RX2, RX3, OUT,
+    src_hbm, tgt_hbm, core_hbm, slw_hbm, tlw_hbm,
+    OUT,
+    src_ref, tgt_ref, core_ref, slw_ref, tlw_ref, load,
+    S, proj, M, T, FB, FS, GS, RXF, RXG, W, CB, RX1, RX2, RX3,
     fsend, frecv, gsend, grecv, s1, r1, s2, r2, s3, r3, s4, r4, s5, r5, s6, r6,
 ):
     si, ti = lax.axis_index("src"), lax.axis_index("tgt")
@@ -39,12 +39,23 @@
     def tgt_peers():
         return [lax.rem(ti + k, n_tgt) for k in range(1, n_tgt)]
 
+    loads = [
+        pltpu.make_async_copy(a, b, load.at[k])
+        for k, (a, b) in enumerate(
+            [(core_hbm, core_ref), (src_hbm, src_ref), (tgt_hbm, tgt_ref), (slw_hbm, slw_ref), (tlw_hbm, tlw_ref)]
+        )
+    ]
+    for copy in loads:
+        copy.start()
+
     barrier = pltpu.get_barrier_semaphore()
     for p in src_peers():
         pl.semaphore_signal(barrier, inc=1, device_id=(p, ti), device_id_type=MESH)
     for p in tgt_peers():
         pl.semaphore_signal(barrier, inc=1, device_id=(si, p), device_id_type=MESH)
 
+    loads[0].wait()
+    loads[1].wait()
     c32 = core_ref[...]
     c0 = c32.astype(bf16)
     left = c32 - c0.astype(f32)
@@ -56,20 +67,19 @@
         return lax.dot_general(a, b, (((da,), (db,)), ((), ())), preferred_element_type=f32)
 
     proj[...] = (
-        contract(src, c0, 0, 0) + (contract(src, c1, 0, 0) + contract(src, c2, 0, 0))
-    ).astype(bf16)
-
-    M[...] = jnp.full((rows, LANES), -jnp.inf, f32)
-    wide = 2 * LANES
-
-    def score_tile(t, carry):
-        at = pl.ds(pl.multiple_of(t * wide, wide), wide)
+        contract(c0, src, 0, 0) + (contract(c1, src, 0, 0) + contract(c2, src, 0, 0))
+    ).T.astype(bf16)
+    for copy in loads[2:]:
+        copy.wait()
+
+    wide = 4 * LANES
+    for t in range(cols // wide):
+        at = slice(t * wide, (t + 1) * wide)
         y = jnp.dot(proj[...], tgt_ref[:, at], preferred_element_type=f32) * LOG2E
         S[:, at] = y
-        M[...] = jnp.maximum(M[...], jnp.maximum(y[:, :LANES], y[:, LANES:]))
-        return carry
-
-    lax.fori_loop(0, cols // wide, score_tile, 0)
+        parts = [y[:, k : k + LANES] for k in range(0, wide, LANES)]
+        top = functools.reduce(jnp.maximum, parts)
+        M[...] = top if t == 0 else jnp.maximum(M[...], top)
 
     def groups(body, carry, unroll):
         def step(i, carry):
@@ -96,8 +106,7 @@
         for c in range(rc):
             FB[tile(c), :] = jnp.broadcast_to(dense[c : c + 1, :], (LANES, LANES)).T
 
-    def exchange(buf, step, me, peers, send, recv, where):
-        copies = []
+    def exchange(buf, step, me, peers, send, recv, where, meanwhile):
         for k, p in enumerate(peers):
             copy = pltpu.make_async_remote_copy(
                 src_ref=buf.at[step, me],
@@ -108,7 +117,9 @@
                 device_id_type=MESH,
             )
             copy.start()
-            copies.append(copy)
+            pending.append(copy)
+        if meanwhile is not None:
+            meanwhile()
         for k, p in enumerate(peers):
             pltpu.make_async_remote_copy(
                 src_ref=buf.at[step, p],
@@ -118,15 +129,14 @@
                 device_id=where(p),
                 device_id_type=MESH,
             ).wait_recv()
-        return copies
-
-    def share_rows(step):
+
+    def share_rows(step, meanwhile=None):
         RXF[step, ti] = FS[...]
-        return exchange(RXF, step, ti, tgt_peers(), fsend, frecv, lambda p: (si, p))
-
-    def share_cols(step):
+        exchange(RXF, step, ti, tgt_peers(), fsend, frecv, lambda p: (si, p), meanwhile)
+
+    def share_cols(step, meanwhile=None):
         RXG[step, si] = GS[...]
-        return exchange(RXG, step, si, src_peers(), gsend, grecv, lambda p: (p, ti))
+        exchange(RXG, step, si, src_peers(), gsend, grecv, lambda p: (p, ti), meanwhile)
 
     def lse_of(buf, step, n):
         parts = [buf[step, k] for k in range(n)]
@@ -142,7 +152,7 @@
         top = jnp.max(mt, axis=0, keepdims=True)
         FS[c : c + 1, :] = top + jnp.log2(jnp.sum(st * jnp.exp2(mt - top), axis=0, keepdims=True))
     pl.semaphore_wait(barrier, (n_src - 1) + (n_tgt - 1))
-    pending += share_rows(0)
+    share_rows(0)
     f1 = slw - lse_of(RXF, 0, n_tgt)
     to_columns(f1)
 
@@ -170,7 +180,7 @@
     for t in range(cc):
         GS[t : t + 1, :] = jnp.sum(acc[t], axis=0, keepdims=True)
     GS[...] = cm + (jnp.log2(GS[...]) - SHIFT)
-    pending += share_cols(0)
+    share_cols(0)
     g = tlw - lse_of(RXG, 0, n_src)
     v = jnp.exp2(cm + g)
 
@@ -187,42 +197,47 @@
         groups(later_rows, 0, 4)
         for c in range(rc):
             FS[c : c + 1, :] = jnp.sum(T[tile(c), :].T, axis=0, keepdims=True)
-        pending += share_rows(step)
-        move = slw + (SHIFT - jnp.log2(sum(RXF[step, k] for k in range(n_tgt))))
-        u = jnp.exp2(move)
-        to_columns(u)
+        share_rows(step)
+        move = slw - jnp.log2(sum(RXF[step, k] for k in range(n_tgt)))
+        to_columns(jnp.exp2(move))
+        last = step == ITERS - 1
 
         def later_cols(r, acc):
             ub = FB[r, :]
-            return tuple(a + S[r, tile(t)] * ub for t, a in enumerate(acc))
+            new = []
+            for t, a in enumerate(acc):
+                e = S[r, tile(t)] * ub
+                if last:
+                    S[r, tile(t)] = e
+                new.append(a + e)
+            return tuple(new)
 
         acc = groups(later_cols, zeros, 4)
         for t in range(cc):
             GS[t : t + 1, :] = jnp.sum(acc[t], axis=0, keepdims=True)
         GS[...] = GS[...] * v
-        pending += share_cols(step)
-        g = g + (tlw + (SHIFT - jnp.log2(sum(RXG[step, k] for k in range(n_src)))))
+
+        def source_sums():
+            for t in range(0, cols, 2 * LANES):
+                at = slice(t, t + 2 * LANES)
+                W[:, at] = jnp.dot(src_ref[...], S[:, at].astype(bf16), preferred_element_type=f32)
+
+        share_cols(step, source_sums if last else None)
+        g = g + (tlw - jnp.log2(sum(RXG[step, k] for k in range(n_src))))
         v = jnp.exp2(cm + g)
 
-    f_out[...] = (f1 + move) * LN2
-    g_out[...] = g * LN2
-
-    to_columns(u * (2.0 ** -SHIFT))
-    tall = plan.shape[0]
-    tgt = tgt_ref[...]
+    height = CB.shape[0]
+    OUT[height : height + rc, :] = (f1 + (move + SHIFT)) * LN2
+    OUT[height + rc : height + rc + cc, :] = g * LN2
+
     total = None
-    for c in range(rows // tall):
-        at = slice(c * tall, (c + 1) * tall)
-        ub = FB[at, :]
-        for t in range(cc):
-            plan[:, tile(t)] = (S[at, tile(t)] * ub * v[t : t + 1, :]).astype(bf16)
-        panel = contract(plan[...], tgt, 1, 1)
-        high = panel.astype(bf16)
-        low = (panel - high.astype(f32)).astype(bf16)
-        words = src_ref[:, at]
-        part = jnp.dot(words, high, preferred_element_type=f32) + jnp.dot(
-            words, low, preferred_element_type=f32
-        )
+    for t in range(0, cc, 4):
+        at = slice(t * LANES, (t + 4) * LANES)
+        x = jnp.concatenate([W[:, tile(k)] * v[k : k + 1, :] for k in range(t, t + 4)], axis=1)
+        high = x.astype(bf16)
+        low = (x - high.astype(f32)).astype(bf16)
+        words = tgt_ref[:, at]
+        part = contract(high, words, 1, 1) + contract(low, words, 1, 1)
         total = part if total is None else total + part
 
     full, rest = dim // LANES, dim % LANES
@@ -239,7 +254,6 @@
             base = full * line + k * short
             CB[base : base + short, :] = S[tile(k), 0:LANES].T[0:short, :]
 
-    height = CB.shape[0]
     core_id, zi, nz = lax.rem(ti, 2), lax.div(ti, 2), n_tgt // 2
     half = height // 2
     quart = half // n_src
@@ -297,20 +311,27 @@
     gather(si, src_peers(), half_at, quart, s5, r5, on_src)
     gather(core_id, [1 - core_id], 0, half, s6, r6, lambda p: mate)
 
-    scale = dim / (rows * n_src)
+    for copy in pending:
+        copy.wait_send()
+
+
+def unpack(scale, dim, height, lines, f_out, g_out, core_out):
+    rc, cc = f_out.shape[0], g_out.shape[0]
+    f_out[...] = lines[height : height + rc, :]
+    g_out[...] = lines[height + rc : height + rc + cc, :]
+    full, rest = dim // LANES, dim % LANES
+    line = -(-dim // 8) * 8
+    short = -(-rest // 8) * 8
     for t in range(full):
-        core_out[:, tile(t)] = OUT[t * line : t * line + dim, :] * scale
+        core_out[:, tile(t)] = lines[t * line : t * line + dim, :] * scale
     if rest:
         for k in range(-(-dim // LANES)):
             base = full * line + k * short
-            CB_rows = jnp.concatenate(
-                [OUT[base : base + short, :], jnp.zeros((LANES - short, LANES), f32)], axis=0
+            block = jnp.concatenate(
+                [lines[base : base + short, :], jnp.zeros((LANES - short, LANES), jnp.float32)], axis=0
             ).T * scale
             count = min(LANES, dim - k * LANES)
-            core_out[k * LANES : k * LANES + count, full * LANES :] = CB_rows[0:count, 0:rest]
-
-    for copy in pending:
-        copy.wait_send()
+            core_out[k * LANES : k * LANES + count, full * LANES :] = block[0:count, 0:rest]
 
 
 def per_device(n_src, n_tgt, src_emb_t, tgt_emb_t, core, src_logw, tgt_logw):
@@ -327,16 +348,19 @@
     sems = pltpu.SemaphoreType.DMA
     vmem = pl.BlockSpec(memory_space=pltpu.VMEM)
     rc, cc = rows // LANES, cols // LANES
-    f, g, new = pl.pallas_call(
+    hbm = pl.BlockSpec(memory_space=pltpu.HBM)
+    lines = pl.pallas_call(
         functools.partial(kernel, n_src, n_tgt),
-        out_shape=(
-            jax.ShapeDtypeStruct((rc, LANES), f32),
-            jax.ShapeDtypeStruct((cc, LANES), f32),
-            jax.ShapeDtypeStruct((dim, dim), f32),
-        ),
-        in_specs=[vmem] * 5,
-        out_specs=(vmem,) * 3,
+        out_shape=jax.ShapeDtypeStruct((height + rc + cc, LANES), f32),
+        in_specs=[hbm] * 5,
+        out_specs=vmem,
         scratch_shapes=[
+            pltpu.VMEM(src_emb_t.shape, jnp.bfloat16),
+            pltpu.VMEM(tgt_emb_t.shape, jnp.bfloat16),
+            pltpu.VMEM(core.shape, f32),
+            pltpu.VMEM((rc, LANES), f32),
+            pltpu.VMEM((cc, LANES), f32),
+            sems((5,)),
             pltpu.VMEM((rows, cols), f32),
             pltpu.VMEM((rows, dim), jnp.bfloat16),
             pltpu.VMEM((rows, LANES), f32),
@@ -346,12 +370,11 @@
             pltpu.VMEM((cc, LANES), f32),
             pltpu.VMEM((ITERS, n_tgt, rc, LANES), f32),
             pltpu.VMEM((ITERS, n_src, cc, LANES), f32),
-            pltpu.VMEM((256, cols), jnp.bfloat16),
+            pltpu.VMEM((dim, cols), f32),
             pltpu.VMEM((height, LANES), f32),
             pltpu.VMEM((half, LANES), f32),
             pltpu.VMEM((n_src, quart, LANES), f32),
             pltpu.VMEM((nz, quart // nz, LANES), f32),
-            pltpu.VMEM((height, LANES), f32),
             sems((ITERS, n_tgt)), sems((ITERS, n_tgt)),
             sems((ITERS, n_src)), sems((ITERS, n_src)),
             sems, sems,
@@ -362,9 +385,20 @@
             sems((2,)), sems((2,)),
         ],
         compiler_params=pltpu.CompilerParams(
-            collective_id=0, has_side_effects=True, vmem_limit_bytes=48 * 1024 * 1024
+            collective_id=0, has_side_effects=True, vmem_limit_bytes=64 * 1024 * 1024
         ),
     )(src_emb_t, tgt_emb_t, core, src_logw.reshape(rc, LANES), tgt_logw.reshape(cc, LANES))
+    f, g, new = pl.pallas_call(
+        functools.partial(unpack, dim / (rows * n_src), dim, height),
+        out_shape=(
+            jax.ShapeDtypeStruct((rc, LANES), f32),
+            jax.ShapeDtypeStruct((cc, LANES), f32),
+            jax.ShapeDtypeStruct((dim, dim), f32),
+        ),
+        in_specs=[vmem],
+        out_specs=(vmem,) * 3,
+        compiler_params=pltpu.CompilerParams(vmem_limit_bytes=64 * 1024 * 1024),
+    )(lines)
     return f.reshape(rows), g.reshape(cols), new
 
 

time: 68.2 us -> 61.9 us (0.908)
  local copies, waits for them, and re-layouts: 6.73 us -> 0 us
    unnamed x13 -> x0, local copies, waits for them, and re-layouts: 6.73 us -> none
    pallas_call x1 -> x2, Pallas kernels: 60.4 us -> 61 us  [the longest x1 59.1 us: per_device(): pl.pallas_call(functools.partial(kernel, n_src, n_tgt), out_shape=jax.Sha...]
where the time goes in v2:
time: 61.9 us; the launch traced here: 61.7 us
  Pallas kernels  61 us (99%)
  between operations  0.64 us (1%)
    pallas_call x1, Pallas kernels, per_device(): pl.pallas_call(functools.partial(kernel, n_src, n_tgt), out_shape=jax.Sha...  59.1 us
    pallas_call x1, Pallas kernels, per_device(): pl.pallas_call(functools.partial(unpack, dim / (rows * n_src), dim, heigh...  1.89 us

profile of v2, /device:TPU:0, one launch (start us, length us, event | category | flops | bytes accessed | tf_op | source)
XLA Modules:
  0.0 61.7 jit_solution(8296313701219126739)
XLA Ops:
  0.6 59.1 %shard_map.76.lines = f32[792,128]{1,0:T(8,128)} custom-call(bf16[300,1024]{1,0:T(8,128)(2,1)} %src_hbm.1, bf16[300,2048]{1,0:T(8,128)(2,1)} %tgt_hbm.1, f32[300,300]{1,0:T(8,128)} %core_hbm.1, f32[8,128]{1,0:T(8,128)} %bitcast.5, f32[16,128]{1,0:T(8,128)} %bitcast.4), custom_call_target="tpu_custom_call" | custom-call | tf_op jit(solution)/shard_map/pallas_call | solution.py:352
  59.8 1.9 %shard_map.77 = (f32[8,128]{1,0:T(8,128)}, f32[16,128]{1,0:T(8,128)}, f32[300,300]{1,0:T(8,128)}) custom-call(f32[792,128]{1,0:T(8,128)} %shard_map.76.lines), custom_call_target="tpu_custom_call" | custom-call | tf_op jit(solution)/shard_map/pallas_call | solution.py:391

commit v3 on v2

--- a/solution.py
+++ b/solution.py
@@ -24,8 +24,8 @@
     src_hbm, tgt_hbm, core_hbm, slw_hbm, tlw_hbm,
     OUT,
     src_ref, tgt_ref, core_ref, slw_ref, tlw_ref, load,
-    S, proj, M, T, FB, FS, GS, RXF, RXG, W, CB, RX1, RX2, RX3,
-    fsend, frecv, gsend, grecv, s1, r1, s2, r2, s3, r3, s4, r4, s5, r5, s6, r6,
+    S, proj, M, T, FB, FS, GS, RXF, RXG, W, CB, RX1, RX2a, RX3a, RX2b, RX3b,
+    fsend, frecv, gsend, grecv, s1, r1, s2, r2,
 ):
     si, ti = lax.axis_index("src"), lax.axis_index("tgt")
     dim, rows = src_ref.shape
@@ -58,16 +58,14 @@
     loads[1].wait()
     c32 = core_ref[...]
     c0 = c32.astype(bf16)
-    left = c32 - c0.astype(f32)
-    c1 = left.astype(bf16)
-    c2 = (left - c1.astype(f32)).astype(bf16)
+    c1 = (c32 - c0.astype(f32)).astype(bf16)
     src = src_ref[...]
 
     def contract(a, b, da, db):
         return lax.dot_general(a, b, (((da,), (db,)), ((), ())), preferred_element_type=f32)
 
     proj[...] = (
-        contract(c0, src, 0, 0) + (contract(c1, src, 0, 0) + contract(c2, src, 0, 0))
+        contract(c0, src, 0, 0) + contract(c1, src, 0, 0)
     ).T.astype(bf16)
     for copy in loads[2:]:
         copy.wait()
@@ -234,10 +232,7 @@
     for t in range(0, cc, 4):
         at = slice(t * LANES, (t + 4) * LANES)
         x = jnp.concatenate([W[:, tile(k)] * v[k : k + 1, :] for k in range(t, t + 4)], axis=1)
-        high = x.astype(bf16)
-        low = (x - high.astype(f32)).astype(bf16)
-        words = tgt_ref[:, at]
-        part = contract(high, words, 1, 1) + contract(low, words, 1, 1)
+        part = contract(x.astype(bf16), tgt_ref[:, at], 1, 1)
         total = part if total is None else total + part
 
     full, rest = dim // LANES, dim % LANES
@@ -256,11 +251,10 @@
 
     core_id, zi, nz = lax.rem(ti, 2), lax.div(ti, 2), n_tgt // 2
     half = height // 2
-    quart = half // n_src
-    piece = quart // nz
-    half_at = core_id * half
-    quart_at = half_at + si * quart
-    piece_at = quart_at + zi * piece
+    mate = (si, zi * 2 + (1 - core_id))
+    on_src = (n_src, si, src_peers(), lambda p: (p, ti))
+    on_z = (nz, zi, [lax.rem(zi + k, nz) for k in range(1, nz)], lambda p: (si, p * 2 + core_id))
+    streams = [(0, half * 2 // 3, on_src, on_z, RX2a, RX3a), (half * 2 // 3, half // 3, on_z, on_src, RX2b, RX3b)]
 
     def span(start, size):
         return pl.ds(pl.multiple_of(start, 8), size)
@@ -271,45 +265,74 @@
             device_id=where, device_id_type=MESH,
         )
 
-    mate = (si, zi * 2 + (1 - core_id))
-    z_peers = [lax.rem(zi + k, nz) for k in range(1, nz)]
-    on_z = lambda p: (si, p * 2 + core_id)
-    on_src = lambda p: (p, ti)
-
-    copy = remote(CB.at[span((1 - core_id) * half, half)], RX1, s1, r1, mate)
-    copy.start()
-    copy.wait_recv()
-    pending.append(copy)
-    CB[span(half_at, half), :] += RX1[...]
-
-    def scatter(n, me, peers, base, size, RX, send, recv, where):
+    def post(source, dest, send, recv, where):
+        copy = remote(source, dest, send, recv, where)
+        copy.start()
+        pending.append(copy)
+
+    for w, (start, size, *_) in enumerate(streams):
+        theirs = span((1 - core_id) * half + start, size)
+        post(CB.at[theirs], RX1.at[start : start + size], s1.at[w], r1.at[w], mate)
+
+    def post_scatter(w, stage, group, base, size, RX):
+        n, me, peers, where = group
         for k, p in enumerate(peers):
-            copy = remote(CB.at[span(base + p * size, size)], RX.at[me], send.at[k], recv.at[me], where(p))
-            copy.start()
-            pending.append(copy)
+            post(CB.at[span(base + p * size, size)], RX.at[me], s2.at[w, stage, k], r2.at[w, stage, me], where(p))
+
+    def end_scatter(w, stage, group, base, size, RX):
+        n, me, peers, where = group
+        own = CB[span(base + me * size, size), :]
         for k, p in enumerate(peers):
-            remote(RX.at[p], RX.at[p], send.at[k], recv.at[p], where(p)).wait_recv()
-        own = CB[span(base + me * size, size), :]
-        for p in peers:
+            remote(RX.at[p], RX.at[p], s2.at[w, stage, k], r2.at[w, stage, p], where(p)).wait_recv()
             own = own + RX[p]
         return own
 
-    CB[span(quart_at, quart), :] = scatter(n_src, si, src_peers(), half_at, quart, RX2, s2, r2, on_src)
-    OUT[span(piece_at, piece), :] = scatter(nz, zi, z_peers, quart_at, piece, RX3, s3, r3, on_z)
-
-    def gather(me, peers, base, size, send, recv, where):
+    def post_gather(w, stage, group, base, size):
+        n, me, peers, where = group
+        at = span(base + me * size, size)
         for k, p in enumerate(peers):
-            at = span(base + me * size, size)
-            copy = remote(OUT.at[at], OUT.at[at], send.at[k], recv.at[me], where(p))
-            copy.start()
-            pending.append(copy)
-        for k, p in enumerate(peers):
-            at = span(base + p * size, size)
-            remote(OUT.at[at], OUT.at[at], send.at[k], recv.at[p], where(p)).wait_recv()
-
-    gather(zi, z_peers, quart_at, piece, s4, r4, on_z)
-    gather(si, src_peers(), half_at, quart, s5, r5, on_src)
-    gather(core_id, [1 - core_id], 0, half, s6, r6, lambda p: mate)
+            post(OUT.at[at], OUT.at[at], s2.at[w, stage, k], r2.at[w, stage, me], where(p))
+
+    def wait_block(w, stage, k, p, at, where):
+        remote(OUT.at[at], OUT.at[at], s2.at[w, stage, k], r2.at[w, stage, p], where).wait_recv()
+
+    plans = []
+    for w, (start, size, first, second, RXa, RXb) in enumerate(streams):
+        base = core_id * half + start
+        block = size // first[0]
+        block_at = base + first[1] * block
+        piece = block // second[0]
+        plans.append((base, block, block_at, piece))
+        at = span(base, size)
+        remote(CB.at[at], RX1.at[start : start + size], s1.at[w], r1.at[w], mate).wait_recv()
+        CB[at, :] += RX1[start : start + size, :]
+        post_scatter(w, 0, first, base, block, RXa)
+    for w, (start, size, first, second, RXa, RXb) in enumerate(streams):
+        base, block, block_at, piece = plans[w]
+        CB[span(block_at, block), :] = end_scatter(w, 0, first, base, block, RXa)
+        post_scatter(w, 1, second, block_at, piece, RXb)
+    for w, (start, size, first, second, RXa, RXb) in enumerate(streams):
+        base, block, block_at, piece = plans[w]
+        OUT[span(block_at + second[1] * piece, piece), :] = end_scatter(w, 1, second, block_at, piece, RXb)
+        post_gather(w, 2, second, block_at, piece)
+    for w, (start, size, first, second, RXa, RXb) in enumerate(streams):
+        base, block, block_at, piece = plans[w]
+        for k, p in enumerate(second[2]):
+            wait_block(w, 2, k, p, span(block_at + p * piece, piece), second[3](p))
+        post_gather(w, 3, first, base, block)
+        at = span(block_at, block)
+        post(OUT.at[at], OUT.at[at], s2.at[w, 4, first[0] - 1], r2.at[w, 4, first[1]], mate)
+    for w, (start, size, first, second, RXa, RXb) in enumerate(streams):
+        base, block, block_at, piece = plans[w]
+        for k, p in enumerate(first[2]):
+            at = span(base + p * block, block)
+            wait_block(w, 3, k, p, at, first[3](p))
+            post(OUT.at[at], OUT.at[at], s2.at[w, 4, k], r2.at[w, 4, p], mate)
+    for w, (start, size, first, second, RXa, RXb) in enumerate(streams):
+        base, block, block_at, piece = plans[w]
+        for p in range(first[0]):
+            at = span((1 - core_id) * half + start + p * block, block)
+            wait_block(w, 4, p, p, at, mate)
 
     for copy in pending:
         copy.wait_send()
@@ -340,11 +363,11 @@
     f32 = jnp.float32
     line, short = -(-dim // 8) * 8, -(-(dim % LANES) // 8) * 8
     need = (dim // LANES) * line + -(-dim // LANES) * short
-    step = 8 * n_src * n_tgt
-    height = -(-need // step) * step
-    half = height // 2
-    quart = half // n_src
     nz = n_tgt // 2
+    unit = 8 * n_src * nz
+    half = -(-need // (6 * unit)) * 3 * unit
+    height = 2 * half
+    long, brief = half * 2 // 3, half // 3
     sems = pltpu.SemaphoreType.DMA
     vmem = pl.BlockSpec(memory_space=pltpu.VMEM)
     rc, cc = rows // LANES, cols // LANES
@@ -373,16 +396,14 @@
             pltpu.VMEM((dim, cols), f32),
             pltpu.VMEM((height, LANES), f32),
             pltpu.VMEM((half, LANES), f32),
-            pltpu.VMEM((n_src, quart, LANES), f32),
-            pltpu.VMEM((nz, quart // nz, LANES), f32),
+            pltpu.VMEM((n_src, long // n_src, LANES), f32),
+            pltpu.VMEM((nz, long // (n_src * nz), LANES), f32),
+            pltpu.VMEM((nz, brief // nz, LANES), f32),
+            pltpu.VMEM((n_src, brief // (n_src * nz), LANES), f32),
             sems((ITERS, n_tgt)), sems((ITERS, n_tgt)),
             sems((ITERS, n_src)), sems((ITERS, n_src)),
-            sems, sems,
-            sems((n_src,)), sems((n_src,)),
-            sems((nz,)), sems((nz,)),
-            sems((nz,)), sems((nz,)),
-            sems((n_src,)), sems((n_src,)),
             sems((2,)), sems((2,)),
+            sems((2, 5, max(n_src, nz))), sems((2, 5, max(n_src, nz))),
         ],
         compiler_params=pltpu.CompilerParams(
             collective_id=0, has_side_effects=True, vmem_limit_bytes=64 * 1024 * 1024

time: 61.9 us -> 59.9 us (0.968)
  Pallas kernels: 61 us -> 59.1 us
    pallas_call x1, Pallas kernels: 59.1 us -> 57.2 us  [per_device(): pl.pallas_call(functools.partial(kernel, n_src, n_tgt), out_shape=jax.Sha...]
where the time goes in v3:
time: 59.9 us; the launch traced here: 59.7 us
  Pallas kernels  59.1 us (99%)
  between operations  0.64 us (1%)
    pallas_call x1, Pallas kernels, per_device(): pl.pallas_call(functools.partial(kernel, n_src, n_tgt), out_shape=jax.Sha...  57.2 us
    pallas_call x1, Pallas kernels, per_device(): pl.pallas_call(functools.partial(unpack, dim / (rows * n_src), dim, heigh...  1.89 us

profile of v3, /device:TPU:0, one launch (start us, length us, event | category | flops | bytes accessed | tf_op | source)
XLA Modules:
  0.0 59.7 jit_solution(1508009023536339611)
XLA Ops:
  0.6 57.2 %shard_map.76.lines = f32[792,128]{1,0:T(8,128)} custom-call(bf16[300,1024]{1,0:T(8,128)(2,1)} %src_hbm.1, bf16[300,2048]{1,0:T(8,128)(2,1)} %tgt_hbm.1, f32[300,300]{1,0:T(8,128)} %core_hbm.1, f32[8,128]{1,0:T(8,128)} %bitcast.5, f32[16,128]{1,0:T(8,128)} %bitcast.4), custom_call_target="tpu_custom_call" | custom-call | tf_op jit(solution)/shard_map/pallas_call | solution.py:375
  57.9 1.9 %shard_map.77 = (f32[8,128]{1,0:T(8,128)}, f32[16,128]{1,0:T(8,128)}, f32[300,300]{1,0:T(8,128)}) custom-call(f32[792,128]{1,0:T(8,128)} %shard_map.76.lines), custom_call_target="tpu_custom_call" | custom-call | tf_op jit(solution)/shard_map/pallas_call | solution.py:412

commit v4 on v3

v4 whole, which is shorter than its diff:
```python
import functools

import jax
import jax.numpy as jnp
from jax import lax
from jax.experimental import pallas as pl
from jax.experimental.pallas import tpu as pltpu
from jax.sharding import PartitionSpec as P

ITERS = 3
BLOCKS = 2
LOG2E = 1.4426950408889634
LN2 = 0.6931471805599453
LANES = 128
SHIFT = 60.0
MESH = pl.DeviceIdType.MESH


def tile(t):
    return slice(t * LANES, (t + 1) * LANES)


def kernel(
    n_src, n_tgt,
    src_hbm, tgt_hbm, core_hbm, slw_hbm, tlw_hbm,
    OUT,
    src_ref, tgt_ref, core_ref, slw_ref, tlw_ref, load,
    S, proj, M, T, FB, FS, GS, RXF, RXG, W, CB, RX1, RX2a, RX3a, RX2b, RX3b,
    fsend, frecv, gsend, grecv, s1, r1, s2, r2,
):
    si, ti = lax.axis_index("src"), lax.axis_index("tgt")
    dim, rows = src_ref.shape
    cols = tgt_ref.shape[1]
    rc, cc = rows // LANES, cols // LANES
    f32, bf16 = jnp.float32, jnp.bfloat16

    def src_peers():
        return [lax.rem(si + k, n_src) for k in range(1, n_src)]

    def tgt_peers():
        return [lax.rem(ti + k, n_tgt) for k in range(1, n_tgt)]

    loads = [
        pltpu.make_async_copy(a, b, load.at[k])
        for k, (a, b) in enumerate(
            [(core_hbm, core_ref), (src_hbm, src_ref), (tgt_hbm, tgt_ref), (slw_hbm, slw_ref), (tlw_hbm, tlw_ref)]
        )
    ]
    for copy in loads:
        copy.start()

    barrier = pltpu.get_barrier_semaphore()
    for p in src_peers():
        pl.semaphore_signal(barrier, inc=1, device_id=(p, ti), device_id_type=MESH)
    for p in tgt_peers():
        pl.semaphore_signal(barrier, inc=1, device_id=(si, p), device_id_type=MESH)

    loads[0].wait()
    loads[1].wait()
    c32 = core_ref[...]
    c0 = c32.astype(bf16)
    c1 = (c32 - c0.astype(f32)).astype(bf16)
    src = src_ref[...]

    def contract(a, b, da, db):
        return lax.dot_general(a, b, (((da,), (db,)), ((), ())), preferred_element_type=f32)

    proj[...] = (
        contract(c0, src, 0, 0) + contract(c1, src, 0, 0)
    ).T.astype(bf16)
    for copy in loads[2:]:
        copy.wait()

    blocks = range(BLOCKS)
    tall, bc = rows // BLOCKS, rc // BLOCKS
    wide = 4 * LANES
    pending, old = [], []

    def groups(b, body, carry, unroll):
        def step(i, carry):
            for k in range(unroll):
                at = b * tall + (i * unroll + k) * 8
                carry = body(pl.ds(pl.multiple_of(at, 8), 8), carry)
            return carry

        return lax.fori_loop(0, tall // (8 * unroll), step, carry)

    def broadcast_down(line):
        return jnp.broadcast_to(line, (8, LANES))

    def block_tile(b, c):
        return slice(b * tall + c * LANES, b * tall + (c + 1) * LANES)

    def to_columns(b, dense):
        for c in range(bc):
            FB[block_tile(b, c), :] = jnp.broadcast_to(dense[c : c + 1, :], (LANES, LANES)).T

    def add_up(parts):
        while len(parts) > 1:
            parts = [a + b for a, b in zip(parts[::2], parts[1::2])]
        return parts[0]

    def post_all(buf, me, peers, send, recv, where):
        for p in peers:
            pltpu.make_async_remote_copy(
                src_ref=buf.at[me], dst_ref=buf.at[me], send_sem=send, recv_sem=recv,
                device_id=where(p), device_id_type=MESH,
            ).start()

    def whole_wait(ref, send, recv, where):
        return pltpu.make_async_remote_copy(
            src_ref=ref, dst_ref=ref, send_sem=send, recv_sem=recv, device_id=where, device_id_type=MESH
        )

    mate = (si, ti + 1 - 2 * lax.rem(ti, 2))

    def post_rows(step, b):
        RXF[step, b, ti] = FS[b]
        post_all(RXF.at[step, b], ti, tgt_peers(), fsend.at[step, b], frecv.at[step, b], lambda p: (si, p))

    def rows_wait(step, b):
        ref = RXF.at[step, b, pl.ds(0, n_tgt - 1)]
        return whole_wait(ref, fsend.at[step, b], frecv.at[step, b], mate)

    def post_cols(step):
        RXG[step, si] = GS[...]
        post_all(RXG.at[step], si, src_peers(), gsend.at[step], grecv.at[step], lambda p: (p, ti))

    def cols_wait(step):
        return whole_wait(RXG.at[step, pl.ds(0, n_src - 1)], gsend.at[step], grecv.at[step], mate)

    def lse(parts):
        top = functools.reduce(jnp.maximum, parts)
        return top + jnp.log2(sum(jnp.exp2(x - top) for x in parts))

    slw = slw_ref[...] * LOG2E
    tlw = tlw_ref[...] * LOG2E

    def slw_of(b):
        return slw[b * bc : (b + 1) * bc, :]

    for b in blocks:
        mine = slice(b * tall, (b + 1) * tall)
        for t in range(cols // wide):
            at = slice(t * wide, (t + 1) * wide)
            y = jnp.dot(proj[mine, :], tgt_ref[:, at], preferred_element_type=f32) * LOG2E
            S[mine, at] = y
            top = functools.reduce(jnp.maximum, [y[:, k : k + LANES] for k in range(0, wide, LANES)])
            M[mine, :] = top if t == 0 else jnp.maximum(M[mine, :], top)

        def first_rows(r, carry):
            m = M[r, :]
            T[r, :] = add_up([jnp.exp2(S[r, tile(t)] - m) for t in range(cc)])
            return carry

        groups(b, first_rows, 0, 4)
        for c in range(bc):
            mt, st = M[block_tile(b, c), :].T, T[block_tile(b, c), :].T
            top = jnp.max(mt, axis=0, keepdims=True)
            FS[b, c : c + 1, :] = top + jnp.log2(jnp.sum(st * jnp.exp2(mt - top), axis=0, keepdims=True))
        if b == 0:
            pl.semaphore_wait(barrier, (n_src - 1) + (n_tgt - 1))
        post_rows(0, b)

    zeros = tuple(jnp.zeros((8, LANES), f32) for t in range(cc))
    f1, peaks, sums = [], [], []
    for b in blocks:
        rows_wait(0, b).wait_recv()
        f1.append(slw_of(b) - lse([RXF[0, b, k] for k in range(n_tgt)]))
        to_columns(b, f1[b])

        def peak_cols(r, acc):
            fb = FB[r, :]
            return tuple(jnp.maximum(a, S[r, tile(t)] + fb) for t, a in enumerate(acc))

        acc = groups(b, peak_cols, tuple(jnp.full((8, LANES), -jnp.inf, f32) for t in range(cc)), 4)
        for t in range(cc):
            GS[t : t + 1, :] = jnp.max(acc[t], axis=0, keepdims=True)
        peaks.append(GS[...])
        less = [broadcast_down(SHIFT - peaks[b][t : t + 1, :]) for t in range(cc)]

        def first_cols(r, acc):
            fb = FB[r, :]
            new = []
            for t, a in enumerate(acc):
                e = jnp.exp2(S[r, tile(t)] + fb + less[t])
                S[r, tile(t)] = e
                new.append(a + e)
            return tuple(new)

        acc = groups(b, first_cols, zeros, 2)
        for t in range(cc):
            GS[t : t + 1, :] = jnp.sum(acc[t], axis=0, keepdims=True)
        sums.append(peaks[b] + (jnp.log2(GS[...]) - SHIFT))
    GS[...] = lse(sums)
    post_cols(0)
    for b in blocks:
        rows_wait(0, b).wait_send()
    cols_wait(0).wait_recv()
    g = tlw - lse([RXG[0, k] for k in range(n_src)])
    v = [jnp.exp2(peaks[b] + g) for b in blocks]

    for step in range(1, ITERS):
        last = step == ITERS - 1
        for b in blocks:
            vb = [broadcast_down(v[b][t : t + 1, :]) for t in range(cc)]

            def later_rows(r, carry):
                T[r, :] = add_up([S[r, tile(t)] * vb[t] for t in range(cc)])
                return carry

            groups(b, later_rows, 0, 4)
            for c in range(bc):
                FS[b, c : c + 1, :] = jnp.sum(T[block_tile(b, c), :].T, axis=0, keepdims=True)
            post_rows(step, b)
        cols_wait(step - 1).wait_send()
        moves, sums = [], []
        for b in blocks:
            rows_wait(step, b).wait_recv()
            moves.append(slw_of(b) - jnp.log2(sum(RXF[step, b, k] for k in range(n_tgt))))
            to_columns(b, jnp.exp2(moves[b]))

            def later_cols(r, acc):
                ub = FB[r, :]
                new = []
                for t, a in enumerate(acc):
                    e = S[r, tile(t)] * ub
                    if last:
                        S[r, tile(t)] = e
                    new.append(a + e)
                return tuple(new)

            acc = groups(b, later_cols, zeros, 4)
            for t in range(cc):
                GS[t : t + 1, :] = jnp.sum(acc[t], axis=0, keepdims=True)
            sums.append(GS[...] * v[b])
        GS[...] = sum(sums)
        post_cols(step)
        for b in blocks:
            rows_wait(step, b).wait_send()
        if last:
            peak = functools.reduce(jnp.maximum, peaks)
            ratio = [jnp.exp2(peaks[b] - peak) for b in blocks]
            for t in range(0, cc, 2):
                at = slice(t * LANES, (t + 2) * LANES)
                whole = jnp.concatenate(
                    [
                        jnp.concatenate(
                            [
                                (S[b * tall : (b + 1) * tall, tile(k)] * ratio[b][k : k + 1, :]).astype(bf16)
                                for b in blocks
                            ],
                            axis=0,
                        )
                        for k in (t, t + 1)
                    ],
                    axis=1,
                )
                W[:, at] = jnp.dot(src_ref[...], whole, preferred_element_type=f32)
        cols_wait(step).wait_recv()
        g = g + (tlw - jnp.log2(sum(RXG[step, k] for k in range(n_src))))
        if not last:
            v = [jnp.exp2(peaks[b] + g) for b in blocks]

    end = jnp.exp2(peak + g)
    total = None
    for t in range(0, cc, 4):
        at = slice(t * LANES, (t + 4) * LANES)
        x = jnp.concatenate([W[:, tile(k)] * end[k : k + 1, :] for k in range(t, t + 4)], axis=1)
        part = contract(x.astype(bf16), tgt_ref[:, at], 1, 1)
        total = part if total is None else total + part

    height = CB.shape[0]
    full, rest = dim // LANES, dim % LANES
    line = -(-dim // 8) * 8
    short = -(-rest // 8) * 8
    CB[...] = jnp.zeros(CB.shape, f32)
    for t in range(full):
        CB[t * line : t * line + dim, :] = total[:, tile(t)]
    if rest:
        plan_rows = -(-dim // LANES) * LANES
        S[0:plan_rows, 0:LANES] = jnp.zeros((plan_rows, LANES), f32)
        S[0:dim, 0:rest] = total[:, full * LANES :]
        for k in range(plan_rows // LANES):
            base = full * line + k * short
            CB[base : base + short, :] = S[tile(k), 0:LANES].T[0:short, :]

    core_id, zi, nz = lax.rem(ti, 2), lax.div(ti, 2), n_tgt // 2
    half = height // 2
    on_src = (n_src, si, src_peers(), lambda p: (p, ti))
    on_z = (nz, zi, [lax.rem(zi + k, nz) for k in range(1, nz)], lambda p: (si, p * 2 + core_id))
    streams = [(0, half * 2 // 3, on_src, on_z, RX2a, RX3a), (half * 2 // 3, half // 3, on_z, on_src, RX2b, RX3b)]

    def span(start, size):
        return pl.ds(pl.multiple_of(start, 8), size)

    def post(source, dest, send, recv, where):
        copy = pltpu.make_async_remote_copy(
            src_ref=source, dst_ref=dest, send_sem=send, recv_sem=recv, device_id=where, device_id_type=MESH
        )
        copy.start()
        return copy

    for w, (start, size, *_) in enumerate(streams):
        theirs = span((1 - core_id) * half + start, size)
        pending.append(post(CB.at[theirs], RX1.at[start : start + size], s1.at[w], r1.at[w], mate))
    cols_wait(ITERS - 1).wait_send()
    OUT[height : height + rc, :] = (
        jnp.concatenate([f1[b] + moves[b] for b in blocks], axis=0) + SHIFT
    ) * LN2
    OUT[height + rc : height + rc + cc, :] = g * LN2

    def post_scatter(w, stage, group, base, size, RX):
        n, me, peers, where = group
        for p in peers:
            post(CB.at[span(base + p * size, size)], RX.at[me], s2.at[w, stage], r2.at[w, stage], where(p))
        return whole_wait(RX.at[pl.ds(0, n - 1)], s2.at[w, stage], r2.at[w, stage], mate)

    def post_gather(w, stage, group, base, size):
        n, me, peers, where = group
        at = span(base + me * size, size)
        for p in peers:
            post(OUT.at[at], OUT.at[at], s2.at[w, stage], r2.at[w, stage], where(p))
        return whole_wait(OUT.at[pl.ds(0, (n - 1) * size)], s2.at[w, stage], r2.at[w, stage], mate)

    def own_sum(group, base, size, RX):
        n, me, peers, where = group
        own = CB[span(base + me * size, size), :]
        for p in peers:
            own = own + RX[p]
        return own

    plans, waits = [], []
    for w, (start, size, first, second, RXa, RXb) in enumerate(streams):
        base = core_id * half + start
        block = size // first[0]
        block_at = base + first[1] * block
        piece = block // second[0]
        plans.append((base, block, block_at, piece))
        at = span(base, size)
        pending[w].wait_recv()
        CB[at, :] += RX1[start : start + size, :]
        waits.append(post_scatter(w, 0, first, base, block, RXa))
    for copy in pending:
        copy.wait_send()
    for w, (start, size, first, second, RXa, RXb) in enumerate(streams):
        base, block, block_at, piece = plans[w]
        waits[w].wait_recv()
        CB[span(block_at, block), :] = own_sum(first, base, block, RXa)
        old.append(waits[w])
        waits[w] = post_scatter(w, 1, second, block_at, piece, RXb)
    for copy in old:
        copy.wait_send()
    old = []
    for w, (start, size, first, second, RXa, RXb) in enumerate(streams):
        base, block, block_at, piece = plans[w]
        waits[w].wait_recv()
        OUT[span(block_at + second[1] * piece, piece), :] = own_sum(second, block_at, piece, RXb)
        old.append(waits[w])
        waits[w] = post_gather(w, 2, second, block_at, piece)
    for copy in old:
        copy.wait_send()
    old = []
    for w, (start, size, first, second, RXa, RXb) in enumerate(streams):
        base, block, block_at, piece = plans[w]
        waits[w].wait_recv()
        old.append(waits[w])
        waits[w] = post_gather(w, 3, first, base, block)
    for copy in old:
        copy.wait_send()
    final = []
    for w, (start, size, first, second, RXa, RXb) in enumerate(streams):
        base, block, block_at, piece = plans[w]
        waits[w].wait_recv()
        at = span(base, size)
        final.append(post(OUT.at[at], OUT.at[at], s2.at[w, 4], r2.at[w, 4], mate))
    for copy in waits:
        copy.wait_send()
    for copy in final:
        copy.wait()


def unpack(scale, dim, height, lines, f_out, g_out, core_out):
    rc, cc = f_out.shape[0], g_out.shape[0]
    f_out[...] = lines[height : height + rc, :]
    g_out[...] = lines[height + rc : height + rc + cc, :]
    full, rest = dim // LANES, dim % LANES
    line = -(-dim // 8) * 8
    short = -(-rest // 8) * 8
    for t in range(full):
        core_out[:, tile(t)] = lines[t * line : t * line + dim, :] * scale
    if rest:
        for k in range(-(-dim // LANES)):
            base = full * line + k * short
            block = jnp.concatenate(
                [lines[base : base + short, :], jnp.zeros((LANES - short, LANES), jnp.float32)], axis=0
            ).T * scale
            count = min(LANES, dim - k * LANES)
            core_out[k * LANES : k * LANES + count, full * LANES :] = block[0:count, 0:rest]


def per_device(n_src, n_tgt, src_emb_t, tgt_emb_t, core, src_logw, tgt_logw):
    dim, rows = src_emb_t.shape
    cols = tgt_emb_t.shape[1]
    f32 = jnp.float32
    line, short = -(-dim // 8) * 8, -(-(dim % LANES) // 8) * 8
    need = (dim // LANES) * line + -(-dim // LANES) * short
    nz = n_tgt // 2
    unit = 8 * n_src * nz
    half = -(-need // (6 * unit)) * 3 * unit
    height = 2 * half
    long, brief = half * 2 // 3, half // 3
    sems = pltpu.SemaphoreType.DMA
    vmem = pl.BlockSpec(memory_space=pltpu.VMEM)
    rc, cc = rows // LANES, cols // LANES
    hbm = pl.BlockSpec(memory_space=pltpu.HBM)
    lines = pl.pallas_call(
        functools.partial(kernel, n_src, n_tgt),
        out_shape=jax.ShapeDtypeStruct((height + rc + cc, LANES), f32),
        in_specs=[hbm] * 5,
        out_specs=vmem,
        scratch_shapes=[
            pltpu.VMEM(src_emb_t.shape, jnp.bfloat16),
            pltpu.VMEM(tgt_emb_t.shape, jnp.bfloat16),
            pltpu.VMEM(core.shape, f32),
            pltpu.VMEM((rc, LANES), f32),
            pltpu.VMEM((cc, LANES), f32),
            sems((5,)),
            pltpu.VMEM((rows, cols), f32),
            pltpu.VMEM((rows, dim), jnp.bfloat16),
            pltpu.VMEM((rows, LANES), f32),
            pltpu.VMEM((rows, LANES), f32),
            pltpu.VMEM((rows, LANES), f32),
            pltpu.VMEM((BLOCKS, rc // BLOCKS, LANES), f32),
            pltpu.VMEM((cc, LANES), f32),
            pltpu.VMEM((ITERS, BLOCKS, n_tgt, rc // BLOCKS, LANES), f32),
            pltpu.VMEM((ITERS, n_src, cc, LANES), f32),
            pltpu.VMEM((dim, cols), f32),
            pltpu.VMEM((height, LANES), f32),
            pltpu.VMEM((half, LANES), f32),
            pltpu.VMEM((n_src, long // n_src, LANES), f32),
            pltpu.VMEM((nz, long // (n_src * nz), LANES), f32),
            pltpu.VMEM((nz, brief // nz, LANES), f32),
            pltpu.VMEM((n_src, brief // (n_src * nz), LANES), f32),
            sems((ITERS, BLOCKS)), sems((ITERS, BLOCKS)),
            sems((ITERS,)), sems((ITERS,)),
            sems((2,)), sems((2,)),
            sems((2, 5)), sems((2, 5)),
        ],
        compiler_params=pltpu.CompilerParams(
            collective_id=0, has_side_effects=True, vmem_limit_bytes=64 * 1024 * 1024
        ),
    )(src_emb_t, tgt_emb_t, core, src_logw.reshape(rc, LANES), tgt_logw.reshape(cc, LANES))
    f, g, new = pl.pallas_call(
        functools.partial(unpack, dim / (rows * n_src), dim, height),
        out_shape=(
            jax.ShapeDtypeStruct((rc, LANES), f32),
            jax.ShapeDtypeStruct((cc, LANES), f32),
            jax.ShapeDtypeStruct((dim, dim), f32),
        ),
        in_specs=[vmem],
        out_specs=(vmem,) * 3,
        compiler_params=pltpu.CompilerParams(vmem_limit_bytes=64 * 1024 * 1024),
    )(lines)
    return f.reshape(rows), g.reshape(cols), new


def solution(mesh):
    placed = (P(None, "src"), P(None, "tgt"), P(), P("src"), P("tgt"))
    body = functools.partial(per_device, mesh.shape["src"], mesh.shape["tgt"])
    return jax.shard_map(
        body, mesh=mesh, in_specs=placed, out_specs=(P("src"), P("tgt"), P()), check_vma=False
    )
```

time: 59.9 us -> 56.7 us (0.947)
  Pallas kernels: 59.1 us -> 55.9 us
    pallas_call x1, Pallas kernels: 57.2 us -> 54 us  [per_device(): pl.pallas_call(functools.partial(kernel, n_src, n_tgt), out_shape=jax.Sha...]
where the time goes in v4:
time: 56.7 us; the launch traced here: 56.6 us
  Pallas kernels  55.9 us (99%)
  between operations  0.64 us (1%)
    pallas_call x1, Pallas kernels, per_device(): pl.pallas_call(functools.partial(kernel, n_src, n_tgt), out_shape=jax.Sha...  54 us
    pallas_call x1, Pallas kernels, per_device(): pl.pallas_call(functools.partial(unpack, dim / (rows * n_src), dim, heigh...  1.89 us

profile of v4, /device:TPU:0, one launch (start us, length us, event | category | flops | bytes accessed | tf_op | source)
XLA Modules:
  0.0 56.6 jit_solution(2004901210205151521)
XLA Ops:
  0.6 54.0 %shard_map.76.lines = f32[792,128]{1,0:T(8,128)} custom-call(bf16[300,1024]{1,0:T(8,128)(2,1)} %src_hbm.1, bf16[300,2048]{1,0:T(8,128)(2,1)} %tgt_hbm.1, f32[300,300]{1,0:T(8,128)} %core_hbm.1, f32[8,128]{1,0:T(8,128)} %bitcast.5, f32[16,128]{1,0:T(8,128)} %bitcast.4), custom_call_target="tpu_custom_call" | custom-call | tf_op jit(solution)/shard_map/pallas_call | solution.py:417
  54.7 1.9 %shard_map.77 = (f32[8,128]{1,0:T(8,128)}, f32[16,128]{1,0:T(8,128)}, f32[300,300]{1,0:T(8,128)}) custom-call(f32[792,128]{1,0:T(8,128)} %shard_map.76.lines), custom_call_target="tpu_custom_call" | custom-call | tf_op jit(solution)/shard_map/pallas_call | solution.py:454

commit v5 on v4

--- a/solution.py
+++ b/solution.py
@@ -1,4 +1,5 @@
 import functools
+import math
 
 import jax
 import jax.numpy as jnp
@@ -25,8 +26,8 @@
     src_hbm, tgt_hbm, core_hbm, slw_hbm, tlw_hbm,
     OUT,
     src_ref, tgt_ref, core_ref, slw_ref, tlw_ref, load,
-    S, proj, M, T, FB, FS, GS, RXF, RXG, W, CB, RX1, RX2a, RX3a, RX2b, RX3b,
-    fsend, frecv, gsend, grecv, s1, r1, s2, r2,
+    S, proj, M, T, FB, FS, GS, RXF, RXG, W, CB, RX2a, RX3a, RX2b, RX3b,
+    fsend, frecv, gsend, grecv, s2, r2,
 ):
     si, ti = lax.axis_index("src"), lax.axis_index("tgt")
     dim, rows = src_ref.shape
@@ -49,9 +50,11 @@
     for copy in loads:
         copy.start()
 
+    mate = (si, ti + 1 - 2 * lax.rem(ti, 2))
     barrier = pltpu.get_barrier_semaphore()
     for p in src_peers():
         pl.semaphore_signal(barrier, inc=1, device_id=(p, ti), device_id_type=MESH)
+        pl.semaphore_signal(barrier, inc=1, device_id=(p, mate[1]), device_id_type=MESH)
     for p in tgt_peers():
         pl.semaphore_signal(barrier, inc=1, device_id=(si, p), device_id_type=MESH)
 
@@ -74,7 +77,6 @@
     blocks = range(BLOCKS)
     tall, bc = rows // BLOCKS, rc // BLOCKS
     wide = 4 * LANES
-    pending, old = [], []
 
     def groups(b, body, carry, unroll):
         def step(i, carry):
@@ -111,8 +113,6 @@
         return pltpu.make_async_remote_copy(
             src_ref=ref, dst_ref=ref, send_sem=send, recv_sem=recv, device_id=where, device_id_type=MESH
         )
-
-    mate = (si, ti + 1 - 2 * lax.rem(ti, 2))
 
     def post_rows(step, b):
         RXF[step, b, ti] = FS[b]
@@ -159,7 +159,7 @@
             top = jnp.max(mt, axis=0, keepdims=True)
             FS[b, c : c + 1, :] = top + jnp.log2(jnp.sum(st * jnp.exp2(mt - top), axis=0, keepdims=True))
         if b == 0:
-            pl.semaphore_wait(barrier, (n_src - 1) + (n_tgt - 1))
+            pl.semaphore_wait(barrier, 2 * (n_src - 1) + (n_tgt - 1))
         post_rows(0, b)
 
     zeros = tuple(jnp.zeros((8, LANES), f32) for t in range(cc))
@@ -286,98 +286,70 @@
             CB[base : base + short, :] = S[tile(k), 0:LANES].T[0:short, :]
 
     core_id, zi, nz = lax.rem(ti, 2), lax.div(ti, 2), n_tgt // 2
-    half = height // 2
-    on_src = (n_src, si, src_peers(), lambda p: (p, ti))
-    on_z = (nz, zi, [lax.rem(zi + k, nz) for k in range(1, nz)], lambda p: (si, p * 2 + core_id))
-    streams = [(0, half * 2 // 3, on_src, on_z, RX2a, RX3a), (half * 2 // 3, half // 3, on_z, on_src, RX2b, RX3b)]
+    on_src = [(p, m) for p in [si] + src_peers() for m in (ti, mate[1])][1:]
+    on_z = [(si, p) for p in tgt_peers()]
+    over_src = [(p, ti) for p in src_peers()]
+    over_z = [(si, lax.rem(zi + k, nz) * 2 + core_id) for k in range(1, nz)]
+
+    def by_plane(d):
+        return d[0] * 2 + lax.rem(d[1], 2)
+
+    def by_column(d):
+        return d[1]
+
+    long = height * 2 // 3
+    streams = [
+        (0, long // (2 * n_src), 2 * n_src, on_src, by_plane, nz, over_z, zi, RX2a, RX3a),
+        (long, (height - long) // n_tgt, n_tgt, on_z, by_column, n_src, over_src, si, RX2b, RX3b),
+    ]
 
     def span(start, size):
         return pl.ds(pl.multiple_of(start, 8), size)
 
     def post(source, dest, send, recv, where):
-        copy = pltpu.make_async_remote_copy(
+        pltpu.make_async_remote_copy(
             src_ref=source, dst_ref=dest, send_sem=send, recv_sem=recv, device_id=where, device_id_type=MESH
-        )
-        copy.start()
-        return copy
-
-    for w, (start, size, *_) in enumerate(streams):
-        theirs = span((1 - core_id) * half + start, size)
-        pending.append(post(CB.at[theirs], RX1.at[start : start + size], s1.at[w], r1.at[w], mate))
-    cols_wait(ITERS - 1).wait_send()
+        ).start()
+
+    waits, old = [], [cols_wait(ITERS - 1)]
+    for w, (start, size, n, peers, index, n2, peers2, me2, RXa, RXb) in enumerate(streams):
+        me = index((si, ti))
+        for d in peers:
+            at = span(start + index(d) * size, size)
+            post(CB.at[at], RXa.at[me], s2.at[w, 0], r2.at[w, 0], d)
+        waits.append(whole_wait(RXa.at[pl.ds(0, n - 1)], s2.at[w, 0], r2.at[w, 0], mate))
     OUT[height : height + rc, :] = (
         jnp.concatenate([f1[b] + moves[b] for b in blocks], axis=0) + SHIFT
     ) * LN2
     OUT[height + rc : height + rc + cc, :] = g * LN2
-
-    def post_scatter(w, stage, group, base, size, RX):
-        n, me, peers, where = group
-        for p in peers:
-            post(CB.at[span(base + p * size, size)], RX.at[me], s2.at[w, stage], r2.at[w, stage], where(p))
-        return whole_wait(RX.at[pl.ds(0, n - 1)], s2.at[w, stage], r2.at[w, stage], mate)
-
-    def post_gather(w, stage, group, base, size):
-        n, me, peers, where = group
-        at = span(base + me * size, size)
-        for p in peers:
-            post(OUT.at[at], OUT.at[at], s2.at[w, stage], r2.at[w, stage], where(p))
-        return whole_wait(OUT.at[pl.ds(0, (n - 1) * size)], s2.at[w, stage], r2.at[w, stage], mate)
-
-    def own_sum(group, base, size, RX):
-        n, me, peers, where = group
-        own = CB[span(base + me * size, size), :]
-        for p in peers:
-            own = own + RX[p]
-        return own
-
-    plans, waits = [], []
-    for w, (start, size, first, second, RXa, RXb) in enumerate(streams):
-        base = core_id * half + start
-        block = size // first[0]
-        block_at = base + first[1] * block
-        piece = block // second[0]
-        plans.append((base, block, block_at, piece))
-        at = span(base, size)
-        pending[w].wait_recv()
-        CB[at, :] += RX1[start : start + size, :]
-        waits.append(post_scatter(w, 0, first, base, block, RXa))
-    for copy in pending:
-        copy.wait_send()
-    for w, (start, size, first, second, RXa, RXb) in enumerate(streams):
-        base, block, block_at, piece = plans[w]
+    for wait in old:
+        wait.wait_send()
+    old = []
+    for w, (start, size, n, peers, index, n2, peers2, me2, RXa, RXb) in enumerate(streams):
+        own = CB[span(start + index((si, ti)) * size, size), :]
         waits[w].wait_recv()
-        CB[span(block_at, block), :] = own_sum(first, base, block, RXa)
+        for d in peers:
+            own = own + RXa[index(d)]
+        RXb[me2] = own
+        for d in peers2:
+            post(RXb.at[me2], RXb.at[me2], s2.at[w, 1], r2.at[w, 1], d)
         old.append(waits[w])
-        waits[w] = post_scatter(w, 1, second, block_at, piece, RXb)
-    for copy in old:
-        copy.wait_send()
+        waits[w] = whole_wait(RXb.at[pl.ds(0, n2 - 1)], s2.at[w, 1], r2.at[w, 1], mate)
+    for wait in old:
+        wait.wait_send()
     old = []
-    for w, (start, size, first, second, RXa, RXb) in enumerate(streams):
-        base, block, block_at, piece = plans[w]
+    for w, (start, size, n, peers, index, n2, peers2, me2, RXa, RXb) in enumerate(streams):
         waits[w].wait_recv()
-        OUT[span(block_at + second[1] * piece, piece), :] = own_sum(second, block_at, piece, RXb)
+        at = span(start + index((si, ti)) * size, size)
+        OUT[at, :] = sum(RXb[k] for k in range(n2))
+        for d in peers:
+            post(OUT.at[at], OUT.at[at], s2.at[w, 2], r2.at[w, 2], d)
         old.append(waits[w])
-        waits[w] = post_gather(w, 2, second, block_at, piece)
-    for copy in old:
-        copy.wait_send()
-    old = []
-    for w, (start, size, first, second, RXa, RXb) in enumerate(streams):
-        base, block, block_at, piece = plans[w]
-        waits[w].wait_recv()
-        old.append(waits[w])
-        waits[w] = post_gather(w, 3, first, base, block)
-    for copy in old:
-        copy.wait_send()
-    final = []
-    for w, (start, size, first, second, RXa, RXb) in enumerate(streams):
-        base, block, block_at, piece = plans[w]
-        waits[w].wait_recv()
-        at = span(base, size)
-        final.append(post(OUT.at[at], OUT.at[at], s2.at[w, 4], r2.at[w, 4], mate))
-    for copy in waits:
-        copy.wait_send()
-    for copy in final:
-        copy.wait()
+        waits[w] = whole_wait(OUT.at[pl.ds(0, (n - 1) * size)], s2.at[w, 2], r2.at[w, 2], mate)
+    for wait in old:
+        wait.wait_send()
+    for wait in waits:
+        wait.wait()
 
 
 def unpack(scale, dim, height, lines, f_out, g_out, core_out):
@@ -406,10 +378,10 @@
     line, short = -(-dim // 8) * 8, -(-(dim % LANES) // 8) * 8
     need = (dim // LANES) * line + -(-dim // LANES) * short
     nz = n_tgt // 2
-    unit = 8 * n_src * nz
-    half = -(-need // (6 * unit)) * 3 * unit
-    height = 2 * half
-    long, brief = half * 2 // 3, half // 3
+    unit = 16 * math.lcm(n_src, nz)
+    height = -(-need // (3 * unit)) * 3 * unit
+    long = height * 2 // 3
+    block, brief = long // (2 * n_src), (height - long) // n_tgt
     sems = pltpu.SemaphoreType.DMA
     vmem = pl.BlockSpec(memory_space=pltpu.VMEM)
     rc, cc = rows // LANES, cols // LANES
@@ -437,15 +409,13 @@
             pltpu.VMEM((ITERS, n_src, cc, LANES), f32),
             pltpu.VMEM((dim, cols), f32),
             pltpu.VMEM((height, LANES), f32),
-            pltpu.VMEM((half, LANES), f32),
-            pltpu.VMEM((n_src, long // n_src, LANES), f32),
-            pltpu.VMEM((nz, long // (n_src * nz), LANES), f32),
-            pltpu.VMEM((nz, brief // nz, LANES), f32),
-            pltpu.VMEM((n_src, brief // (n_src * nz), LANES), f32),
+            pltpu.VMEM((2 * n_src, block, LANES), f32),
+            pltpu.VMEM((nz, block, LANES), f32),
+            pltpu.VMEM((n_tgt, brief, LANES), f32),
+            pltpu.VMEM((n_src, brief, LANES), f32),
             sems((ITERS, BLOCKS)), sems((ITERS, BLOCKS)),
             sems((ITERS,)), sems((ITERS,)),
-            sems((2,)), sems((2,)),
-            sems((2, 5)), sems((2, 5)),
+            sems((2, 3)), sems((2, 3)),
         ],
         compiler_params=pltpu.CompilerParams(
             collective_id=0, has_side_effects=True, vmem_limit_bytes=64 * 1024 * 1024

time: 56.7 us -> 53 us (0.935)
  Pallas kernels: 55.9 us -> 52.2 us
    pallas_call x1, Pallas kernels: 54 us -> 50.3 us  [per_device(): pl.pallas_call(functools.partial(kernel, n_src, n_tgt), out_shape=jax.Sha...]
where the time goes in v5:
time: 53 us; the launch traced here: 52.8 us
  Pallas kernels  52.2 us (98%)
  between operations  0.64 us (1%)
    pallas_call x1, Pallas kernels, per_device(): pl.pallas_call(functools.partial(kernel, n_src, n_tgt), out_shape=jax.Sha...  50.3 us
    pallas_call x1, Pallas kernels, per_device(): pl.pallas_call(functools.partial(unpack, dim / (rows * n_src), dim, heigh...  1.89 us

profile of v5, /device:TPU:0, one launch (start us, length us, event | category | flops | bytes accessed | tf_op | source)
XLA Modules:
  0.0 52.8 jit_solution(7269376104426105842)
XLA Ops:
  0.6 50.3 %shard_map.76.lines = f32[792,128]{1,0:T(8,128)} custom-call(bf16[300,1024]{1,0:T(8,128)(2,1)} %src_hbm.1, bf16[300,2048]{1,0:T(8,128)(2,1)} %tgt_hbm.1, f32[300,300]{1,0:T(8,128)} %core_hbm.1, f32[8,128]{1,0:T(8,128)} %bitcast.5, f32[16,128]{1,0:T(8,128)} %bitcast.4), custom_call_target="tpu_custom_call" | custom-call | tf_op jit(solution)/shard_map/pallas_call | solution.py:389
  51.0 1.9 %shard_map.77 = (f32[8,128]{1,0:T(8,128)}, f32[16,128]{1,0:T(8,128)}, f32[300,300]{1,0:T(8,128)}) custom-call(f32[792,128]{1,0:T(8,128)} %shard_map.76.lines), custom_call_target="tpu_custom_call" | custom-call | tf_op jit(solution)/shard_map/pallas_call | solution.py:424

commit v6 on v5

--- a/solution.py
+++ b/solution.py
@@ -39,7 +39,8 @@
         return [lax.rem(si + k, n_src) for k in range(1, n_src)]
 
     def tgt_peers():
-        return [lax.rem(ti + k, n_tgt) for k in range(1, n_tgt)]
+        order = sorted(range(1, n_tgt), key=lambda k: abs(k - n_tgt // 2))
+        return [lax.rem(ti + k, n_tgt) for k in order]
 
     loads = [
         pltpu.make_async_copy(a, b, load.at[k])
@@ -239,6 +240,7 @@
         for b in blocks:
             rows_wait(step, b).wait_send()
         if last:
+            CB[...] = jnp.zeros(CB.shape, f32)
             peak = functools.reduce(jnp.maximum, peaks)
             ratio = [jnp.exp2(peaks[b] - peak) for b in blocks]
             for t in range(0, cc, 2):
@@ -262,31 +264,9 @@
         if not last:
             v = [jnp.exp2(peaks[b] + g) for b in blocks]
 
-    end = jnp.exp2(peak + g)
-    total = None
-    for t in range(0, cc, 4):
-        at = slice(t * LANES, (t + 4) * LANES)
-        x = jnp.concatenate([W[:, tile(k)] * end[k : k + 1, :] for k in range(t, t + 4)], axis=1)
-        part = contract(x.astype(bf16), tgt_ref[:, at], 1, 1)
-        total = part if total is None else total + part
-
     height = CB.shape[0]
-    full, rest = dim // LANES, dim % LANES
-    line = -(-dim // 8) * 8
-    short = -(-rest // 8) * 8
-    CB[...] = jnp.zeros(CB.shape, f32)
-    for t in range(full):
-        CB[t * line : t * line + dim, :] = total[:, tile(t)]
-    if rest:
-        plan_rows = -(-dim // LANES) * LANES
-        S[0:plan_rows, 0:LANES] = jnp.zeros((plan_rows, LANES), f32)
-        S[0:dim, 0:rest] = total[:, full * LANES :]
-        for k in range(plan_rows // LANES):
-            base = full * line + k * short
-            CB[base : base + short, :] = S[tile(k), 0:LANES].T[0:short, :]
-
     core_id, zi, nz = lax.rem(ti, 2), lax.div(ti, 2), n_tgt // 2
-    on_src = [(p, m) for p in [si] + src_peers() for m in (ti, mate[1])][1:]
+    on_src = [(p, m) for p in src_peers() for m in (ti, mate[1])] + [mate]
     on_z = [(si, p) for p in tgt_peers()]
     over_src = [(p, ti) for p in src_peers()]
     over_z = [(si, lax.rem(zi + k, nz) * 2 + core_id) for k in range(1, nz)]
@@ -311,13 +291,45 @@
             src_ref=source, dst_ref=dest, send_sem=send, recv_sem=recv, device_id=where, device_id_type=MESH
         ).start()
 
-    waits, old = [], [cols_wait(ITERS - 1)]
-    for w, (start, size, n, peers, index, n2, peers2, me2, RXa, RXb) in enumerate(streams):
+    waits, old = [None, None], [cols_wait(ITERS - 1)]
+
+    def scatter(w):
+        start, size, n, peers, index, n2, peers2, me2, RXa, RXb = streams[w]
         me = index((si, ti))
         for d in peers:
             at = span(start + index(d) * size, size)
             post(CB.at[at], RXa.at[me], s2.at[w, 0], r2.at[w, 0], d)
-        waits.append(whole_wait(RXa.at[pl.ds(0, n - 1)], s2.at[w, 0], r2.at[w, 0], mate))
+        waits[w] = whole_wait(RXa.at[pl.ds(0, n - 1)], s2.at[w, 0], r2.at[w, 0], mate)
+
+    end = jnp.exp2(peak + g)
+    step = 4
+    weighed = [
+        jnp.concatenate([W[:, tile(k)] * end[k : k + 1, :] for k in range(t, t + step)], axis=1).astype(bf16)
+        for t in range(0, cc, step)
+    ]
+
+    def product(low, high):
+        return sum(
+            contract(x, tgt_ref[low:high, k * step * LANES : (k + 1) * step * LANES], 1, 1)
+            for k, x in enumerate(weighed)
+        )
+
+    full, rest = dim // LANES, dim % LANES
+    line = -(-dim // 8) * 8
+    short = -(-rest // 8) * 8
+    right = product(LANES, dim)
+    for t in range(1, full):
+        CB[t * line : t * line + dim, :] = right[:, tile(t - 1)]
+    if rest:
+        plan_rows = -(-dim // LANES) * LANES
+        S[0:plan_rows, 0:LANES] = jnp.zeros((plan_rows, LANES), f32)
+        S[0:dim, 0:rest] = right[:, (full - 1) * LANES :]
+        for k in range(plan_rows // LANES):
+            base = full * line + k * short
+            CB[base : base + short, :] = S[tile(k), 0:LANES].T[0:short, :]
+    scatter(1)
+    CB[0:dim, :] = product(0, LANES)
+    scatter(0)
     OUT[height : height + rc, :] = (
         jnp.concatenate([f1[b] + moves[b] for b in blocks], axis=0) + SHIFT
     ) * LN2

time: 53 us -> 54.5 us (1.028)
  Pallas kernels: 52.2 us -> 53.7 us
    pallas_call x1, Pallas kernels: 50.3 us -> 51.8 us  [per_device(): pl.pallas_call(functools.partial(kernel, n_src, n_tgt), out_shape=jax.Sha...]
where the time goes in v6:
time: 54.5 us; the launch traced here: 54.3 us
  Pallas kernels  53.7 us (99%)
  between operations  0.64 us (1%)
    pallas_call x1, Pallas kernels, per_device(): pl.pallas_call(functools.partial(kernel, n_src, n_tgt), out_shape=jax.Sha...  51.8 us
    pallas_call x1, Pallas kernels, per_device(): pl.pallas_call(functools.partial(unpack, dim / (rows * n_src), dim, heigh...  1.89 us

profile of v6, /device:TPU:0, one launch (start us, length us, event | category | flops | bytes accessed | tf_op | source)
XLA Modules:
  0.0 54.3 jit_solution(860171769194631234)
XLA Ops:
  0.6 51.8 %shard_map.76.lines = f32[792,128]{1,0:T(8,128)} custom-call(bf16[300,1024]{1,0:T(8,128)(2,1)} %src_hbm.1, bf16[300,2048]{1,0:T(8,128)(2,1)} %tgt_hbm.1, f32[300,300]{1,0:T(8,128)} %core_hbm.1, f32[8,128]{1,0:T(8,128)} %bitcast.5, f32[16,128]{1,0:T(8,128)} %bitcast.4), custom_call_target="tpu_custom_call" | custom-call | tf_op jit(solution)/shard_map/pallas_call | solution.py:401
  52.4 1.9 %shard_map.77 = (f32[8,128]{1,0:T(8,128)}, f32[16,128]{1,0:T(8,128)}, f32[300,300]{1,0:T(8,128)}) custom-call(f32[792,128]{1,0:T(8,128)} %shard_map.76.lines), custom_call_target="tpu_custom_call" | custom-call | tf_op jit(solution)/shard_map/pallas_call | solution.py:436

commit v7 on v5

--- a/solution.py
+++ b/solution.py
@@ -39,7 +39,8 @@
         return [lax.rem(si + k, n_src) for k in range(1, n_src)]
 
     def tgt_peers():
-        return [lax.rem(ti + k, n_tgt) for k in range(1, n_tgt)]
+        order = sorted(range(1, n_tgt), key=lambda k: abs(k - n_tgt // 2))
+        return [lax.rem(ti + k, n_tgt) for k in order]
 
     loads = [
         pltpu.make_async_copy(a, b, load.at[k])

time: 53 us -> 53.7 us (1.013)
  Pallas kernels: 52.2 us -> 52.8 us
    pallas_call x1, Pallas kernels: 50.3 us -> 50.9 us  [per_device(): pl.pallas_call(functools.partial(kernel, n_src, n_tgt), out_shape=jax.Sha...]
where the time goes in v7:
time: 53.7 us; the launch traced here: 53.5 us
  Pallas kernels  52.8 us (98%)
  between operations  0.64 us (1%)
    pallas_call x1, Pallas kernels, per_device(): pl.pallas_call(functools.partial(kernel, n_src, n_tgt), out_shape=jax.Sha...  50.9 us
    pallas_call x1, Pallas kernels, per_device(): pl.pallas_call(functools.partial(unpack, dim / (rows * n_src), dim, heigh...  1.89 us

profile of v7, /device:TPU:0, one launch (start us, length us, event | category | flops | bytes accessed | tf_op | source)
XLA Modules:
  0.0 53.5 jit_solution(627961288544676448)
XLA Ops:
  0.6 50.9 %shard_map.76.lines = f32[792,128]{1,0:T(8,128)} custom-call(bf16[300,1024]{1,0:T(8,128)(2,1)} %src_hbm.1, bf16[300,2048]{1,0:T(8,128)(2,1)} %tgt_hbm.1, f32[300,300]{1,0:T(8,128)} %core_hbm.1, f32[8,128]{1,0:T(8,128)} %bitcast.5, f32[16,128]{1,0:T(8,128)} %bitcast.4), custom_call_target="tpu_custom_call" | custom-call | tf_op jit(solution)/shard_map/pallas_call | solution.py:390
  51.6 1.9 %shard_map.77 = (f32[8,128]{1,0:T(8,128)}, f32[16,128]{1,0:T(8,128)}, f32[300,300]{1,0:T(8,128)}) custom-call(f32[792,128]{1,0:T(8,128)} %shard_map.76.lines), custom_call_target="tpu_custom_call" | custom-call | tf_op jit(solution)/shard_map/pallas_call | solution.py:425
